TPU v7x, 128 devices: a whole 4x4x4 slice. The times are simulated.
128 devices in a mesh: dp: 16 (over x, y), ctx: 8 (over z, core).
Axes of the slice: x: 4, y: 4, z: 4, core: 2. Of those that a mesh axis runs over, the one named last changes fastest.
Arguments:
- tokens: bfloat16 [16, 2048, 1024], P('dp', 'ctx'), may hold values from -6 to 6
- cotangent: bfloat16 [16, 2048, 1024], P('dp', 'ctx'), may hold values from -6 to 6
- proj_weight: bfloat16 [1024, 3072], replicated, may hold values from -0.1875 to 0.1875
- segment: int32 [16, 2048], P('dp', 'ctx'), may hold values from 0 to 2, never falling along the last dimension, each value on 1 to 1024 neighbouring positions
Outputs:
- output: bfloat16 [16, 2048, 1024], P('dp', 'ctx')
- grad_tokens: bfloat16 [16, 2048, 1024], P('dp', 'ctx')
- grad_weight: float32 [1024, 3072], replicated
Inputs may be any that keep to these rules, and one draw needn't show every extreme that they name: `segment`: segment numbers never fall along a group's tokens; every history holds 1 to 1024 tokens and one of each group exactly 1024.
All inputs are finite; a program needn't handle non-finite values.
Results may differ from a plain program's by a relative error of at most 0.014.
Values may be sent and summed in bfloat16 or wider, within the bound.
No kernel may reach another device: no remote copies, remote signals or barrier semaphores. Data moves between devices by JAX's collectives and lax.ppermute only.
A program may use at most 128 MiB of HBM per device.

v0:
```python
import jax
import jax.numpy as jnp
from jax import lax
from jax.sharding import PartitionSpec as P

HEADS = 8


EPS = 1e-05


def normalize(value):
    centred = value - jnp.mean(value, axis=-1, keepdims=True)
    spread = jnp.mean(centred * centred, axis=-1, keepdims=True)
    return centred * lax.rsqrt(spread + EPS)


def normalize_back(grad, value):
    centred = value - jnp.mean(value, axis=-1, keepdims=True)
    factor = lax.rsqrt(jnp.mean(centred * centred, axis=-1, keepdims=True) + EPS)
    normal = centred * factor
    inner = grad - jnp.mean(grad, axis=-1, keepdims=True)
    return factor * (inner - normal * jnp.mean(grad * normal, axis=-1, keepdims=True))


def silu_grad(value):
    sigma = jax.nn.sigmoid(value)
    return sigma * (1.0 + value * (1.0 - sigma))


def body(tokens, cotangent, proj_weight, segment):
    x_tok = tokens[0]
    grad_out = cotangent[0]
    seg_ids = segment[0]
    tok_rows = x_tok.shape[0]
    model_width = x_tok.shape[1]
    n_heads = HEADS
    head_size = model_width // n_heads
    ctx_count = lax.axis_size("ctx")
    group_rows = tok_rows * ctx_count
    scale = 1.0 / head_size**0.5
    inv_most = 1.0 / (group_rows // 2)
    inv_root = 1.0 / (lax.axis_size("dp") * group_rows) ** 0.5
    my_index = lax.axis_index("ctx")
    query_places = my_index * tok_rows + jnp.arange(tok_rows, dtype=jnp.int32)
    x_float = x_tok.astype(jnp.float32)
    normed = normalize(x_float).astype(jnp.bfloat16)
    pre_act = jnp.dot(normed, proj_weight, preferred_element_type=jnp.float32)
    activated = jax.nn.silu(pre_act).astype(jnp.bfloat16)
    query = activated[:, :model_width]
    keys = activated[:, model_width : 2 * model_width]
    values = activated[:, 2 * model_width :]
    query_heads = query.reshape(tok_rows, n_heads, head_size)

    def score_block(key_rows, key_seg):
        key_heads = key_rows.reshape(-1, n_heads, head_size)
        scores = (
            jnp.einsum("qhd,khd->hqk", query_heads, key_heads, preferred_element_type=jnp.float32)
            * scale
        )
        key_places = jnp.arange(key_rows.shape[0], dtype=jnp.int32)
        visible = (key_places[None, :] <= query_places[:, None]) & (
            key_seg[None, :] == seg_ids[:, None]
        )
        visible = visible & (key_places[None, :] >= 0)
        return (scores, visible)

    scores, visible = score_block(
        lax.all_gather(keys, "ctx", axis=0, tiled=True),
        lax.all_gather(seg_ids, "ctx", axis=0, tiled=True),
    )
    weights = jnp.where(visible[None], jax.nn.silu(scores) * inv_most, 0.0).astype(jnp.bfloat16)
    value_heads = lax.all_gather(values, "ctx", axis=0, tiled=True).reshape(-1, n_heads, head_size)
    summed = jnp.einsum("hqk,khd->qhd", weights, value_heads, preferred_element_type=jnp.float32)
    attended = summed.reshape(tok_rows, model_width)
    all_keys, all_values, all_seg = (
        lax.all_gather(keys, "ctx", axis=0, tiled=True),
        lax.all_gather(values, "ctx", axis=0, tiled=True),
        lax.all_gather(seg_ids, "ctx", axis=0, tiled=True),
    )
    output = (x_float + normalize(attended)).astype(jnp.bfloat16)
    grad_att = normalize_back(grad_out.astype(jnp.float32), attended).astype(jnp.bfloat16)
    grad_heads = grad_att.reshape(tok_rows, n_heads, head_size)
    scores, visible = score_block(all_keys, all_seg)
    weights = jnp.where(visible[None], jax.nn.silu(scores) * inv_most, 0.0).astype(jnp.bfloat16)
    key_heads = all_keys.reshape(-1, n_heads, head_size)
    value_heads = all_values.reshape(-1, n_heads, head_size)
    grad_prod = jnp.einsum(
        "qhd,khd->hqk", grad_heads, value_heads, preferred_element_type=jnp.float32
    )
    grad_scores = jnp.where(
        visible[None], grad_prod * silu_grad(scores) * (inv_most * scale), 0.0
    ).astype(jnp.bfloat16)
    query_part = jnp.einsum(
        "hqk,khd->qhd", grad_scores, key_heads, preferred_element_type=jnp.float32
    ).reshape(tok_rows, model_width)
    key_part = jnp.einsum(
        "hqk,qhd->khd", grad_scores, query_heads, preferred_element_type=jnp.float32
    ).reshape(-1, model_width)
    value_part = jnp.einsum(
        "hqk,qhd->khd", weights, grad_heads, preferred_element_type=jnp.float32
    ).reshape(-1, model_width)
    grad_keys, grad_values = (
        lax.psum_scatter(
            key_part.astype(jnp.bfloat16), "ctx", scatter_dimension=0, tiled=True
        ).astype(jnp.float32),
        lax.psum_scatter(
            value_part.astype(jnp.bfloat16), "ctx", scatter_dimension=0, tiled=True
        ).astype(jnp.float32),
    )
    joined = jnp.concatenate([query_part, grad_keys, grad_values], axis=1)
    grad_pre = (joined * silu_grad(pre_act)).astype(jnp.bfloat16)
    weight_term = (
        lax.dot_general(
            normed, grad_pre, (((0,), (0,)), ((), ())), preferred_element_type=jnp.float32
        )
        * inv_root
    )
    grad_normed = lax.dot_general(
        grad_pre, proj_weight, (((1,), (1,)), ((), ())), preferred_element_type=jnp.float32
    )
    grad_tok = (grad_out.astype(jnp.float32) + normalize_back(grad_normed, x_float)).astype(
        jnp.bfloat16
    )
    grad_weight = lax.psum(weight_term, ("dp", "ctx"))
    return (output[None], grad_tok[None], grad_weight)


def solution(mesh):
    in_specs = (P("dp", "ctx", None), P("dp", "ctx", None), P(), P("dp", "ctx"))
    out_specs = (P("dp", "ctx", None), P("dp", "ctx", None), P())
    return jax.shard_map(body, mesh=mesh, in_specs=in_specs, out_specs=out_specs, check_vma=False)
```

profile of v0, /device:TPU:1, one launch (start us, length us, event | category | flops | bytes accessed | tf_op | source)
XLA Modules:
  0.0 388.2 jit_solution(3015656942901380621)
XLA Ops:
  7.2 1.2 convert_reduce_fusion
  8.4 1.3 fusion.18
  9.7 6.5 %multiply_convert_fusion = (bf16[256,3072]{1,0:T(8,128)(2,1)S(1)}, f32[256,3072]{1,0:T(8,128)}) fusion(bf16[1024,3072]{1,0:T(8,128)(2,1)} %param.6, bf16[1,256,1024]{2,1,0:T(8,128)(2,1)} %param.4, f32[256]{0:T(256)S(1)} %add_rsqrt_fusion.1, f32[256]{0:T(256)S(1)} %broadcast_multiply_fusion.5), kind=kOutput, calls=%fused_computation.13 | convolution fusion | flops 1615593472 | bytes 11536384 | tf_op jit(solution)/shard_map/dot_general | solution.py:48
  18.4 1.3 copy.11
  19.7 13.3 %all-gather = s32[1,2048]{1,0:T(1,128)S(1)} all-gather(s32[1,256]{1,0:T(1,128)S(1)} %copy-done.5), channel_id=2, replica_groups=mesh['dp'=16,'ctx'=8] {'ctx'}, dimensions={1}, use_global_device_ids=true | all-gather | bytes 9216 | tf_op jit(solution)/shard_map/all_gather | solution.py:70
  33.7 19.8 %all-gather.6.cloned.1.call-done = bf16[2048,1024]{1,0:T(8,128)(2,1)} async-done(((bf16[256,1024]{1,0:T(8,128)(2,1)}), bf16[2048,1024]{1,0:T(8,128)(2,1)}) %all-gather.6.cloned.1.call-update) | async-done | bytes 4194320 | tf_op jit(solution)/shard_map/all_gather | solution.py:69
  53.5 6.5 %copy.25 = bf16[2048,1024]{0,1:T(8,128)(2,1)} copy(bf16[2048,1024]{1,0:T(8,128)(2,1)} %all-gather.6.cloned.1.call-done) | data formatting | bytes 8388608 | tf_op jit(solution)/shard_map/reshape | solution.py:56
  60.0 14.6 %select_convert_fusion.1 = (bf16[8,256,2048]{2,1,0:T(8,128)(2,1)}, f32[8,256,2048]{2,1,0:T(8,128)}) fusion(pred[256,2048]{1,0:T(8,128)(4,1)S(1)} %fusion.6, bf16[256,8,128]{0,2,1:T(8,128)(2,1)S(1)} %bitcast.101, bf16[2048,8,128]{0,2,1:T(8,128)(2,1)} %bitcast.97), kind=kOutput, calls=%fused_computation.1 | convolution fusion | flops 1107296256 | bytes 30408704 | tf_op jit(solution)/shard_map/qhd,khd->hqk/dot_general | solution.py:58
  74.6 13.4 %all-gather.4.cloned.1.call-done = bf16[2048,1024]{1,0:T(8,128)(2,1)} async-done(((bf16[256,1024]{1,0:T(8,128)(2,1)}), bf16[2048,1024]{1,0:T(8,128)(2,1)}) %all-gather.4.cloned.1.call-update) | async-done | bytes 4194320 | tf_op jit(solution)/shard_map/all_gather | solution.py:73
  88.0 7.6 %fusion.27 = (f32[256]{0:T(256)S(1)}, f32[8,128,256]{2,1,0:T(8,128)S(1)}) fusion(bf16[8,256,2048]{2,1,0:T(8,128)(2,1)} %get-tuple-element.10, bf16[2048,1024]{1,0:T(8,128)(2,1)} %all-gather.4.cloned.1.call-done), kind=kOutput, calls=%fused_computation.52 | convolution fusion | flops 1074003712 | bytes 13632512 | tf_op jit(solution)/shard_map/hqk,khd->qhd/dot_general | solution.py:74
  95.8 1.3 copy.12
  97.1 1.6 fusion.20
  98.7 1.5 multiply_convert_fusion.1
  100.2 6.6 %convolution_convert_fusion = bf16[8,128,2048]{2,1,0:T(8,128)(2,1)} fusion(bf16[256,8,128]{0,2,1:T(8,128)(2,1)S(1)} %multiply_convert_fusion.1, bf16[8,256,2048]{2,1,0:T(8,128)(2,1)} %get-tuple-element.10), kind=kOutput, calls=%fused_computation.7 | convolution fusion | flops 1075838976 | bytes 13107200 | tf_op jit(solution)/shard_map/hqk,qhd->khd/dot_general | solution.py:100
  106.8 6.4 %copy.23 = bf16[2048,1024]{1,0:T(8,128)(2,1)} copy(bf16[2048,1024]{0,1:T(8,128)(2,1)} %bitcast.93) | data formatting | bytes 8388608 | tf_op jit(solution)/shard_map/convert_element_type | solution.py:108
  113.5 14.0 %select_convert_fusion = bf16[8,256,2048]{2,1,0:T(8,128)(2,1)S(1)} fusion(f32[8,256,2048]{2,1,0:T(8,128)} %get-tuple-element.11, pred[256,2048]{1,0:T(8,128)(4,1)} %copy-done.4, bf16[256,8,128]{0,2,1:T(8,128)(2,1)S(1)} %multiply_convert_fusion.1, bf16[2048,1024]{1,0:T(8,128)(2,1)} %all-gather.4.cloned.1.call-done), kind=kOutput, calls=%fused_computation | convolution fusion | flops 1124073472 | bytes 30408704 | tf_op jit(solution)/shard_map/qhd,khd->hqk/dot_general | solution.py:88
  127.5 3.7 convolution_convert_fusion.1
  132.1 6.4 %copy.22 = bf16[2048,1024]{1,0:T(8,128)(2,1)} copy(bf16[2048,1024]{0,1:T(8,128)(2,1)} %bitcast.94) | data formatting | bytes 8388608 | tf_op jit(solution)/shard_map/convert_element_type | solution.py:105
  138.9 8.7 %fusion.28 = f32[8,128,256]{2,1,0:T(8,128)} fusion(bf16[2048,8,128]{0,2,1:T(8,128)(2,1)} %bitcast.98, bf16[8,256,2048]{2,1,0:T(8,128)(2,1)} %copy-done), kind=kOutput, calls=%fused_computation.53 | convolution fusion | flops 1073741824 | bytes 13631488 | tf_op jit(solution)/shard_map/hqk,khd->qhd/dot_general | solution.py:94
  147.6 2.6 copy.21
  150.2 2.1 convert_element_type.90
  152.4 34.8 %reduce-scatter.3.cloned.1.call-done = bf16[256,1024]{1,0:T(8,128)(2,1)} async-done(((bf16[2048,1024]{1,0:T(8,128)(2,1)}), bf16[256,1024]{1,0:T(8,128)(2,1)}) %reduce-scatter.3.cloned.1.call-update) | async-done | bytes 524304 | tf_op jit(solution)/shard_map/reduce_scatter | solution.py:104
  187.2 1.1 convert_element_type.86
  188.4 3.1 fusion.5
  191.5 1.2 copy-done.3
  192.7 6.7 %convolution_multiply_fusion = f32[1024,3072]{1,0:T(8,128)} fusion(bf16[256,3072]{1,0:T(8,128)(2,1)S(1)} %fusion.5, bf16[1,256,1024]{2,1,0:T(8,128)(2,1)S(1)} %copy-done.1, f32[256]{0:T(256)S(1)} %add_rsqrt_fusion.1, f32[256]{0:T(256)S(1)} %broadcast_multiply_fusion.5), kind=kOutput, calls=%fused_computation.3 | convolution fusion | flops 1614807040 | bytes 14682112 | tf_op jit(solution)/shard_map/dot_general | solution.py:114
  199.5 1.3 copy.10
  200.8 2.3 fusion.19
  203.1 5.3 %fusion.25 = (f32[256]{0:T(256)S(1)}, f32[256]{0:T(256)S(1)}, f32[256,1024]{1,0:T(8,128)S(1)}) fusion(f32[256]{0:T(256)S(1)} %add_rsqrt_fusion.1, f32[256]{0:T(256)S(1)} %broadcast_multiply_fusion.5, bf16[1,256,1024]{2,1,0:T(8,128)(2,1)S(1)} %copy-done.1, bf16[256,3072]{1,0:T(8,128)(2,1)} %copy-done.3, bf16[1024,3072]{1,0:T(8,128)(2,1)} %param.6), kind=kOutput, calls=%fused_computation.50 | convolution fusion | flops 1612185088 | bytes 9441280 | tf_op jit(solution)/shard_map/dot_general | solution.py:119
  208.3 1.2 fusion.21
  209.6 161.1 %all-reduce.2.cloned.1.call-done = f32[1024,3072]{1,0:T(8,128)} async-done(((f32[1024,3072]{1,0:T(8,128)}), f32[1024,3072]{1,0:T(8,128)}) %all-reduce.2.cloned.1.call-update) | async-done | bytes 12582928 | tf_op jit(solution)/shard_map/psum | solution.py:125
  370.7 11.0 %copy.38 = f32[1024,3072]{1,0:T(8,128)} copy(f32[1024,3072]{1,0:T(8,128)} %all-reduce.2.cloned.1.call-done) | data formatting | bytes 25165824
  (35 shorter events, 4.6 us)
Async XLA Ops:
  7.2 46.4 %all-gather.6.cloned.1.call-start = ((), (), s32[]{:S(2)}) async-start(), calls=%async_computation.3 | async-start | bytes 4718592 | tf_op jit(solution)/shard_map/all_gather | solution.py:69
  16.3 2.1 copy-start.2
  16.3 3.4 copy-start.5
  17.4 70.6 %all-gather.4.cloned.1.call-start = ((), (), s32[]{:S(2)}) async-start(), calls=%async_computation.2 | async-start | bytes 4718592 | tf_op jit(solution)/shard_map/all_gather | solution.py:73
  18.2 132.1 %reduce-scatter.5.cloned.1.call-start = ((), (), s32[]{:S(2)}) async-start(), calls=%async_computation.5 | async-start | bytes 4718592 | tf_op jit(solution)/shard_map/reduce_scatter | solution.py:107
  33.7 26.3 %copy-start.4 = (pred[256,2048]{1,0:T(8,128)(4,1)}, pred[256,2048]{1,0:T(8,128)(4,1)S(1)}, u32[]{:S(2)}) copy-start(pred[256,2048]{1,0:T(8,128)(4,1)S(1)} %fusion.6) | copy-start | bytes 1572868
  113.2 74.0 %reduce-scatter.3.cloned.1.call-start = ((), (), s32[]{:S(2)}) async-start(), calls=%async_computation.4 | async-start | bytes 4718592 | tf_op jit(solution)/shard_map/reduce_scatter | solution.py:104
  127.4 4.7 %copy-start = (bf16[8,256,2048]{2,1,0:T(8,128)(2,1)}, bf16[8,256,2048]{2,1,0:T(8,128)(2,1)S(1)}, u32[]{:S(2)}) copy-start(bf16[8,256,2048]{2,1,0:T(8,128)(2,1)S(1)} %select_convert_fusion) | copy-start | bytes 25165828
  138.6 232.2 %all-reduce.2.cloned.1.call-start = ((), (), s32[]{:S(2)}) async-start(), calls=%async_computation.6 | async-start | bytes 25165824 | tf_op jit(solution)/shard_map/psum | solution.py:125
  188.4 4.4 %copy-start.1 = (bf16[1,256,1024]{2,1,0:T(8,128)(2,1)S(1)}, bf16[1,256,1024]{2,1,0:T(8,128)(2,1)}, u32[]{:S(2)}) copy-start(bf16[1,256,1024]{2,1,0:T(8,128)(2,1)} %param.4) | copy-start | bytes 1572868
  191.5 1.2 copy-start.3
Sparse Core Ops, SparseCore 0:
  17.5 35.9 all-gather.5
  55.8 32.1 all-gather.3
  113.3 34.4 reduce-scatter.4
  150.1 37.0 reduce-scatter.2
  199.6 171.0 all-reduce.1
where the time goes:
time: 389 us; the launch traced here: 388 us
  waiting for transfers between devices  230 us (59%)
  matrix products  73.8 us (19%)
  local copies, waits for them, and re-layouts  40.3 us (10%)
  other arithmetic  16.4 us (4%)
  between operations  13.9 us (4%)
  blocking collectives  13.3 us (3%)
    psum x1, waiting for transfers between devices, body(): grad_weight = lax.psum(weight_term, ('dp', 'ctx'))  161 us
    reduce_scatter x1, waiting for transfers between devices, body(): lax.psum_scatter(key_part.astype(jnp.bfloat16), 'ctx', scatter_dimension=...  34.8 us
    all_gather x1, waiting for transfers between devices, body(): lax.all_gather(keys, 'ctx', axis=0, tiled=True)  19.8 us
    dot_general x1, matrix products, score_block(): jnp.einsum('qhd,khd->hqk', query_heads, key_heads, preferred_element_type...  14.6 us
    dot_general x1, matrix products, body(): jnp.einsum('qhd,khd->hqk', grad_heads, value_heads, preferred_element_typ...  14 us
    all_gather x1, waiting for transfers between devices, body(): lax.all_gather(values, 'ctx', axis=0, tiled=True)  13.4 us
    all_gather x1, blocking collectives, body(): lax.all_gather(seg_ids, 'ctx', axis=0, tiled=True)  13.3 us
    unnamed x13, local copies, waits for them, and re-layouts  13.1 us
  transfers between devices with their start and end apart: 5, of which 4 were waited for; matrix products, arithmetic and copies ran while one was open for 18% of the time, Pallas kernels for 0%

commit v1 on v0

v1 whole, which is shorter than its diff:
```python
import jax
import jax.numpy as jnp
from jax import lax
from jax.experimental import pallas as pl
from jax.experimental.pallas import tpu as pltpu
from jax.sharding import PartitionSpec as P

HEADS = 8
HEAD = 128
EPS = 1e-05
VMEM = 56 * 2**20
F32 = jnp.float32
BF16 = jnp.bfloat16

NN = (((1,), (0,)), ((), ()))
NT = (((1,), (1,)), ((), ()))
TN = (((0,), (0,)), ((), ()))


def dot(a, b, dims=NN):
    return lax.dot_general(a, b, dims, preferred_element_type=F32)


def normalize(value):
    centred = value - jnp.mean(value, axis=-1, keepdims=True)
    spread = jnp.mean(centred * centred, axis=-1, keepdims=True)
    return centred * lax.rsqrt(spread + EPS)


def silu_grad(value):
    half = 0.5 * value
    th = jnp.tanh(half)
    return 0.5 * (1.0 + th) * (1.0 + half * (1.0 - th))


def block_mask(bounds, row0, col0, rows):
    row = row0 + lax.broadcasted_iota(jnp.int32, (rows, 1), 0)
    col = col0 + lax.broadcasted_iota(jnp.int32, (1, rows), 1)
    first = jnp.where(row >= bounds[1], bounds[1], jnp.where(row >= bounds[0], bounds[0], 0))
    return (col <= row) & (col >= first)


def first_block(bounds, row0, rows):
    first = jnp.where(row0 >= bounds[1], bounds[1], jnp.where(row0 >= bounds[0], bounds[0], 0))
    return first // rows


def fwd_kernel(rows, scale, bounds_ref, x_ref, w_ref, cot_ref, normed_ref, pre_ref, act_ref,
               att_ref, stat_ref):
    step = pl.program_id(0)
    bounds = (bounds_ref[0], bounds_ref[1])
    normed = normalize(x_ref[pl.ds(0, rows), :].astype(F32)).astype(BF16)
    normed_ref[...] = normed
    pre = dot(normed, w_ref[...])
    pre_ref[...] = pre
    half = 0.5 * pre
    here = pl.ds(pl.multiple_of(step * rows, rows), rows)
    act_ref[here, :] = (half * (1.0 + jnp.tanh(half))).astype(BF16)
    query = act_ref[here, pl.ds(0, HEAD)]

    def inner(j, total):
        there = pl.ds(pl.multiple_of(j * rows, rows), rows)
        keys = act_ref[there, pl.ds(HEAD, HEAD)]
        values = act_ref[there, pl.ds(2 * HEAD, HEAD)]
        t = dot(query, keys, NT) * (0.5 * scale)
        mask = block_mask(bounds, step * rows, j * rows, rows)
        weights = jnp.where(mask, t * (1.0 + jnp.tanh(t)), 0.0).astype(BF16)
        return total + dot(weights, values)

    att = lax.fori_loop(
        first_block(bounds, step * rows, rows), step + 1, inner, jnp.zeros((rows, HEAD), F32)
    ) * (1.0 / 1024)
    att_t = att.T
    att_ref[...] = att_t
    cot_t = cot_ref[...].astype(F32).T
    mean = jnp.mean(att_t, axis=0, keepdims=True)
    centred = att_t - mean
    stat_ref[...] = jnp.concatenate(
        [
            mean,
            jnp.sum(centred * centred, axis=0, keepdims=True),
            jnp.sum(cot_t * centred, axis=0, keepdims=True),
            jnp.sum(cot_t, axis=0, keepdims=True),
            jnp.zeros((4, rows), F32),
        ],
        axis=0,
    )


def bwd_kernel(rows, scale, inv_root, bounds_ref, act_ref, att_ref, cot_ref, stat_ref, normed_ref,
               pre_ref, out_ref, gw_ref, n_s, dq_s, dk_s, dv_s, gw_s):
    step = pl.program_id(0)
    steps = pl.num_programs(0) // 2
    bounds = (bounds_ref[0], bounds_ref[1])
    width = HEADS * HEAD

    @pl.when(step < steps)
    def _():
        stat = stat_ref[...].reshape(HEADS, 8, rows)
        means, second, cross, sums = stat[:, 0], stat[:, 1], stat[:, 2], stat[:, 3]
        mean = jnp.mean(means, axis=0, keepdims=True)
        shift = means - mean
        var = jnp.sum(second + HEAD * shift * shift, axis=0, keepdims=True) * (1.0 / width)
        factor = lax.rsqrt(var + EPS)
        mean_cot = jnp.sum(sums, axis=0, keepdims=True) * (1.0 / width)
        inner_mean = factor * jnp.sum(cross + shift * sums, axis=0, keepdims=True) * (1.0 / width)
        n_t = (att_ref[...] - mean) * factor
        cot_t = cot_ref[...].astype(F32).T
        ga_t = factor * (cot_t - mean_cot - n_t * inner_mean)
        here = pl.ds(pl.multiple_of(step * rows, rows), rows)
        n_s[here, :] = n_t.T.astype(BF16)
        grad_att = ga_t.T.astype(BF16)
        ga_tb = ga_t.astype(BF16)
        query = act_ref[here, pl.ds(0, HEAD)]
        query_t = query.astype(F32).T.astype(BF16)
        dk_s[step] = jnp.zeros((HEAD, rows), F32)
        dv_s[step] = jnp.zeros((HEAD, rows), F32)

        def inner(j, total):
            there = pl.ds(pl.multiple_of(j * rows, rows), rows)
            keys = act_ref[there, pl.ds(HEAD, HEAD)]
            values = act_ref[there, pl.ds(2 * HEAD, HEAD)]
            t = dot(query, keys, NT) * (0.5 * scale)
            prod = dot(grad_att, values, NT)
            mask = block_mask(bounds, step * rows, j * rows, rows)
            th = jnp.tanh(t)
            up = 1.0 + th
            weights = jnp.where(mask, t * up, 0.0).astype(BF16)
            grads = jnp.where(mask, prod * (up * (1.0 + t * (1.0 - th))), 0.0).astype(BF16)
            dv_s[j] += dot(ga_tb, weights)
            dk_s[j] += dot(query_t, grads)
            return total + dot(grads, keys)

        dq_s[here, :] = lax.fori_loop(
            first_block(bounds, step * rows, rows), step + 1, inner, jnp.zeros((rows, HEAD), F32)
        )

    @pl.when(step >= steps)
    def _():
        block = step - steps
        here = pl.ds(pl.multiple_of(block * rows, rows), rows)
        slope = silu_grad(pre_ref[...])
        inv = 1.0 / 1024
        gpre = jnp.concatenate(
            [
                dq_s[here, :] * (0.5 * inv * scale),
                dk_s[block].T * (0.5 * inv * scale),
                dv_s[block].T * inv,
            ],
            axis=1,
        )
        gpre = (gpre * slope).astype(BF16)
        out_ref[:, pl.ds(0, HEAD)] = n_s[here, :]
        out_ref[:, pl.ds(HEAD, 3 * HEAD)] = gpre
        term = dot(normed_ref[...], gpre, TN)

        @pl.when(block == 0)
        def _():
            gw_s[...] = term

        @pl.when(block > 0)
        def _():
            gw_s[...] += term

        @pl.when(block == steps - 1)
        def _():
            gw_ref[...] = (gw_s[...] * inv_root).astype(BF16)


def out_kernel(rows, got_ref, w_ref, x_ref, cot_ref, out_ref, gtok_ref, g_s, acc_s):
    step = pl.program_id(0)
    width = HEADS * HEAD
    part = w_ref.shape[0]

    @pl.when(step == 0)
    def _():
        for h in range(HEADS):
            out_ref[:, pl.ds(h * HEAD, HEAD)] = (
                x_ref[:, pl.ds(h * HEAD, HEAD)].astype(F32)
                + got_ref[h, :, pl.ds(0, HEAD)].astype(F32)
            ).astype(BF16)
            for t in range(3):
                g_s[:, pl.ds(t * width + h * HEAD, HEAD)] = got_ref[h, :, pl.ds((t + 1) * HEAD, HEAD)]

    acc_s[step] = dot(g_s[...], w_ref[...], NT)

    @pl.when(step == pl.num_programs(0) - 1)
    def _():
        x = x_ref[...].astype(F32)
        centred = x - jnp.mean(x, axis=-1, keepdims=True)
        factor = lax.rsqrt(jnp.mean(centred * centred, axis=-1, keepdims=True) + EPS)
        normal = centred * factor
        grad = jnp.concatenate([acc_s[i] for i in range(width // part)], axis=1)
        back = factor * (
            grad
            - jnp.mean(grad, axis=-1, keepdims=True)
            - normal * jnp.mean(grad * normal, axis=-1, keepdims=True)
        )
        gtok_ref[...] = (cot_ref[...].astype(F32) + back).astype(BF16)


def join_kernel(got_ref, out_ref):
    for h in range(HEADS):
        for t in range(3):
            out_ref[:, pl.ds((t * HEADS + h) * HEAD, HEAD)] = got_ref[
                h, :, pl.ds(t * HEAD, HEAD)
            ].astype(F32)


def params(n):
    return pltpu.CompilerParams(dimension_semantics=("arbitrary",) * n, vmem_limit_bytes=VMEM)


def body(tokens, cotangent, proj_weight, segment):
    x_tok = tokens[0]
    grad_out = cotangent[0]
    seg_ids = segment[0]
    rows, width = x_tok.shape
    ctx_count = lax.axis_size("ctx")
    dp_count = lax.axis_size("dp")
    total = rows * ctx_count
    scale = 1.0 / HEAD**0.5
    inv_root = 1.0 / (dp_count * total) ** 0.5
    head = lax.axis_index("ctx")

    seg_row = jnp.pad(seg_ids.astype(BF16)[None, :], ((0, 15), (0, width - rows)))
    sent = jnp.concatenate([x_tok, seg_row], axis=0)
    shard = sent.shape[0]
    got = lax.all_gather(sent, "ctx", axis=0, tiled=True)
    cot_head = lax.all_to_all(
        grad_out.reshape(rows, HEADS, HEAD).transpose(1, 0, 2), "ctx", 0, 0
    ).reshape(total, HEAD)
    all_seg = got.reshape(ctx_count, shard, width)[:, rows, :rows].astype(F32)
    bounds = jnp.stack([jnp.sum(all_seg < 0.5), jnp.sum(all_seg < 1.5)]).astype(jnp.int32)

    w_head = jnp.concatenate(
        [lax.dynamic_slice_in_dim(proj_weight, t * width + head * HEAD, HEAD, 1) for t in range(3)],
        axis=1,
    )
    normed, pre, act, att_t, stat = pl.pallas_call(
        lambda *refs: fwd_kernel(rows, scale, *refs),
        grid_spec=pltpu.PrefetchScalarGridSpec(
            num_scalar_prefetch=1,
            grid=(ctx_count,),
            in_specs=[
                pl.BlockSpec((shard, width), lambda i, b: (i, 0)),
                pl.BlockSpec((width, 3 * HEAD), lambda i, b: (0, 0)),
                pl.BlockSpec((rows, HEAD), lambda i, b: (i, 0)),
            ],
            out_specs=[
                pl.BlockSpec((rows, width), lambda i, b: (i, 0)),
                pl.BlockSpec((rows, 3 * HEAD), lambda i, b: (i, 0)),
                pl.BlockSpec((total, 3 * HEAD), lambda i, b: (0, 0)),
                pl.BlockSpec((HEAD, rows), lambda i, b: (0, i)),
                pl.BlockSpec((8, rows), lambda i, b: (0, i)),
            ],
        ),
        out_shape=[
            jax.ShapeDtypeStruct((total, width), BF16),
            jax.ShapeDtypeStruct((total, 3 * HEAD), F32),
            jax.ShapeDtypeStruct((total, 3 * HEAD), BF16),
            jax.ShapeDtypeStruct((HEAD, total), F32),
            jax.ShapeDtypeStruct((8, total), F32),
        ],
        compiler_params=params(1),
        name="attend",
    )(bounds, got, w_head, cot_head)

    all_stat = lax.all_gather(stat, "ctx", axis=0, tiled=True)

    late = lambda i: jnp.maximum(i - ctx_count, 0)
    early = lambda i: jnp.minimum(i, ctx_count - 1)
    back, gw = pl.pallas_call(
        lambda *refs: bwd_kernel(rows, scale, inv_root, *refs),
        grid_spec=pltpu.PrefetchScalarGridSpec(
            num_scalar_prefetch=1,
            grid=(2 * ctx_count,),
            in_specs=[
                pl.BlockSpec((total, 3 * HEAD), lambda i, b: (0, 0)),
                pl.BlockSpec((HEAD, rows), lambda i, b: (0, early(i))),
                pl.BlockSpec((rows, HEAD), lambda i, b: (early(i), 0)),
                pl.BlockSpec((8 * HEADS, rows), lambda i, b: (0, early(i))),
                pl.BlockSpec((rows, width), lambda i, b: (late(i), 0)),
                pl.BlockSpec((rows, 3 * HEAD), lambda i, b: (late(i), 0)),
            ],
            out_specs=[
                pl.BlockSpec((rows, 4 * HEAD), lambda i, b: (late(i), 0)),
                pl.BlockSpec((width, 3 * HEAD), lambda i, b: (0, 0)),
            ],
            scratch_shapes=[
                pltpu.VMEM((total, HEAD), BF16),
                pltpu.VMEM((total, HEAD), F32),
                pltpu.VMEM((ctx_count, HEAD, rows), F32),
                pltpu.VMEM((ctx_count, HEAD, rows), F32),
                pltpu.VMEM((width, 3 * HEAD), F32),
            ],
        ),
        out_shape=[
            jax.ShapeDtypeStruct((total, 4 * HEAD), BF16),
            jax.ShapeDtypeStruct((width, 3 * HEAD), BF16),
        ],
        compiler_params=params(1),
        name="attend_back",
    )(bounds, act, att_t, cot_head, all_stat, normed, pre)

    piece = width // dp_count
    terms = lax.all_to_all(gw.reshape(dp_count, piece, 3 * HEAD), "dp", 0, 0)
    summed = jnp.sum(terms.astype(F32), axis=0).astype(BF16)
    pieces = lax.all_gather(summed, ("dp", "ctx"), axis=0, tiled=False)
    grad_weight = pl.pallas_call(
        join_kernel,
        grid=(dp_count,),
        in_specs=[pl.BlockSpec((ctx_count, piece, 3 * HEAD), lambda i: (i, 0, 0))],
        out_specs=pl.BlockSpec((piece, 3 * width), lambda i: (i, 0)),
        out_shape=jax.ShapeDtypeStruct((width, 3 * width), F32),
        compiler_params=params(1),
        name="join",
    )(pieces)

    mine = lax.all_to_all(back.reshape(ctx_count, rows, 4 * HEAD), "ctx", 0, 0)
    part = 256
    output, grad_tok = pl.pallas_call(
        lambda *refs: out_kernel(rows, *refs),
        grid=(width // part,),
        in_specs=[
            pl.BlockSpec((HEADS, rows, 4 * HEAD), lambda i: (0, 0, 0)),
            pl.BlockSpec((part, 3 * width), lambda i: (i, 0)),
            pl.BlockSpec((rows, width), lambda i: (0, 0)),
            pl.BlockSpec((rows, width), lambda i: (0, 0)),
        ],
        out_specs=[
            pl.BlockSpec((rows, width), lambda i: (0, 0)),
            pl.BlockSpec((rows, width), lambda i: (0, 0)),
        ],
        out_shape=[jax.ShapeDtypeStruct((rows, width), BF16)] * 2,
        scratch_shapes=[
            pltpu.VMEM((rows, 3 * width), BF16),
            pltpu.VMEM((width // part, rows, part), F32),
        ],
        compiler_params=params(1),
        name="finish",
    )(mine, proj_weight, x_tok, grad_out)
    return (output[None], grad_tok[None], grad_weight)


def solution(mesh):
    in_specs = (P("dp", "ctx", None), P("dp", "ctx", None), P(), P("dp", "ctx"))
    out_specs = (P("dp", "ctx", None), P("dp", "ctx", None), P())
    return jax.shard_map(body, mesh=mesh, in_specs=in_specs, out_specs=out_specs, check_vma=False)
```

time: 389 us -> 220 us (0.57)
  waiting for transfers between devices: 230 us -> 56 us
  matrix products: 73.8 us -> 0 us
  Pallas kernels: 0 us -> 60.4 us
  blocking collectives: 13.3 us -> 71.4 us
  local copies, waits for them, and re-layouts: 40.3 us -> 3.72 us
  other arithmetic: 16.4 us -> 6.89 us
  starting transfers between devices: 0.68 us -> 6.85 us
    psum x1 -> x0, waiting for transfers between devices: 161 us -> none  [body(): grad_weight = lax.psum(weight_term, ('dp', 'ctx'))]
    dot_general x9 -> x0, matrix products: 73.8 us -> none  [the longest x1 14.6 us: score_block(): jnp.einsum('qhd,khd->hqk', query_heads, key_heads, preferred_element_type...]
    pallas_call x0 -> x4, Pallas kernels: none -> 60.4 us  [the longest x1 22.7 us: body(): pl.pallas_call(lambda *refs: bwd_kernel(rows, scale, inv_root, *refs), gr...]
    all_to_all x0 -> x2, blocking collectives: none -> 57 us  [the longest x1 31.6 us: body(): mine = lax.all_to_all(back.reshape(ctx_count, rows, 4 * HEAD), 'ctx', 0, 0)]
    reduce_scatter x2 -> x0, waiting for transfers between devices: 34.8 us -> none  [the longest x1 34.8 us: body(): lax.psum_scatter(key_part.astype(jnp.bfloat16), 'ctx', scatter_dimension=...]
    all_gather x2, waiting for transfers between devices: 33.2 us -> 56 us  [the longest x1 28.5 us: body(): pieces = lax.all_gather(summed, ('dp', 'ctx'), axis=0, tiled=False)]
    convert_element_type x3 -> x0, local copies, waits for them, and re-layouts: 14.1 us -> none  [the longest x1 6.43 us: body(): key_part.astype(jnp.bfloat16)]
    unnamed x13 -> x7, local copies, waits for them, and re-layouts: 13.1 us -> 0.9 us
  transfers between devices with their start and end apart: 5 -> 3, of which waited for: 4 -> 2; matrix products, arithmetic and copies ran while one was open for 18% -> 3% of each run, Pallas kernels for 0% -> 4%
where the time goes in v1:
time: 220 us; the launch traced here: 219 us
  blocking collectives  71.4 us (32%)
  Pallas kernels  60.4 us (27%)
  waiting for transfers between devices  56 us (25%)
  between operations  14.1 us (6%)
  other arithmetic  6.89 us (3%)
  starting transfers between devices  6.85 us (3%)
  local copies, waits for them, and re-layouts  3.72 us (2%)
    all_to_all x1, blocking collectives, body(): mine = lax.all_to_all(back.reshape(ctx_count, rows, 4 * HEAD), 'ctx', 0, 0)  31.6 us
    all_gather x1, waiting for transfers between devices, body(): pieces = lax.all_gather(summed, ('dp', 'ctx'), axis=0, tiled=False)  28.5 us
    all_gather x1, waiting for transfers between devices, body(): got = lax.all_gather(sent, 'ctx', axis=0, tiled=True)  27.5 us
    all_to_all x1, blocking collectives, body(): terms = lax.all_to_all(gw.reshape(dp_count, piece, 3 * HEAD), 'dp', 0, 0)  25.4 us
    pallas_call x1, Pallas kernels, body(): pl.pallas_call(lambda *refs: bwd_kernel(rows, scale, inv_root, *refs), gr...  22.7 us
    pallas_call x1, Pallas kernels, body(): pl.pallas_call(lambda *refs: fwd_kernel(rows, scale, *refs), grid_spec=pl...  17.5 us
    all_gather x1, blocking collectives, body(): all_stat = lax.all_gather(stat, 'ctx', axis=0, tiled=True)  14.5 us
    pallas_call x1, Pallas kernels, body(): pl.pallas_call(join_kernel, grid=(dp_count,), in_specs=[pl.BlockSpec((ctx...  12.3 us
  transfers between devices with their start and end apart: 3, of which 2 were waited for; matrix products, arithmetic and copies ran while one was open for 3% of the time, Pallas kernels for 4%

profile of v1, /device:TPU:1, one launch (start us, length us, event | category | flops | bytes accessed | tf_op | source)
XLA Modules:
  0.0 219.4 jit_solution(2862714300693211223)
XLA Ops:
  7.2 0.0 copy-start.1
  7.2 0.0 all-gather.4.cloned.1.call-start
  7.2 0.7 convert_element_type.20
  8.0 1.9 fusion.1
  9.8 0.0 all-gather.4.cloned.1.call-update
  9.9 0.0 copy-done.1
  9.9 0.1 copy.11
  10.0 0.9 copy.15
  10.9 6.8 %all-to-all-start = ((bf16[8,256,128]{2,1,0:T(8,128)(2,1)}), bf16[8,256,128]{2,1,0:T(8,128)(2,1)S(1)}, u32[]{:S(2)}, u32[]{:S(2)}) async-start(bf16[8,256,128]{2,1,0:T(8,128)(2,1)} %bitcast.16), calls=%async_computation | async-start | bytes 1048576 | tf_op jit(solution)/shard_map/all_to_all | solution.py:230
  17.7 0.0 all-gather.6.cloned.1.call-start
  17.7 1.2 constant_dynamic-slice_fusion.2
  18.9 1.0 pad_maximum_fusion.refs_2_
  19.9 27.5 %all-gather.4.cloned.1.call-done.refs_1_ = bf16[2176,1024]{1,0:T(8,128)(2,1)} async-done(((bf16[272,1024]{1,0:T(8,128)(2,1)}), bf16[2176,1024]{1,0:T(8,128)(2,1)}) %all-gather.4.cloned.1.call-update) | async-done | bytes 4456464 | tf_op jit(solution)/shard_map/all_gather | solution.py:229
  47.4 0.8 slice.4
  48.1 0.6 convert_reduce_fusion.1
  48.8 1.9 pad_add_fusion.refs_0_
  50.7 0.0 all-to-all-done
  50.7 0.0 copy-start
  50.7 0.8 copy-done
  51.5 17.5 %attend.1 = (bf16[2048,1024]{1,0:T(8,128)(2,1)}, f32[2048,384]{1,0:T(8,128)}, bf16[2048,384]{1,0:T(8,128)(2,1)}, f32[128,2048]{1,0:T(8,128)}, f32[8,2048]{1,0:T(8,128)}) custom-call(s32[2]{0:T(128)} %pad_add_fusion.refs_0_, bf16[2176,1024]{1,0:T(8,128)(2,1)} %all-gather.4.cloned.1.call-done.refs_1_, bf16[1024,384]{1,0:T(8,128)(2,1)} %pad_maximum_fusion.refs_2_, ...), custom_call_target="tpu_custom_call" | custom-call | tf_op jit(solution)/shard_map/attend/pallas_call | solution.py:240
  68.9 14.5 %all_gather.13.refs_4_ = f32[64,2048]{1,0:T(8,128)} all-gather(f32[8,2048]{1,0:T(8,128)} %get-tuple-element.14), channel_id=1, replica_groups=mesh['dp'=16,'ctx'=8] {'ctx'}, dimensions={0}, use_global_device_ids=true | all-gather | bytes 589824 | tf_op jit(solution)/shard_map/all_gather | solution.py:269
  83.4 22.7 %attend_back.1 = (bf16[2048,512]{1,0:T(8,128)(2,1)}, bf16[1024,384]{1,0:T(8,128)(2,1)}) custom-call(s32[2]{0:T(128)} %pad_add_fusion.refs_0_, bf16[2048,384]{1,0:T(8,128)(2,1)} %get-tuple-element.12.refs_1_, f32[128,2048]{1,0:T(8,128)} %get-tuple-element.13.refs_2_, bf16[2048,128]{1,0:T(8,128)(2,1)} %bitcast.19, f32[64,2048]{1,0:T(8,128)} %all_gather.13.refs_4_, ...), custom_call_target="tpu_custom_call" | custom-call | tf_op jit(solution)/shard_map/attend_back/pallas_call | solution.py:273
  106.1 0.0 copy-start.2
  106.1 25.4 %all_to_all.15 = bf16[16,64,384]{2,1,0:T(8,128)(2,1)S(1)} all-to-all(bf16[16,64,384]{2,1,0:T(8,128)(2,1)} %bitcast.27), channel_id=1, replica_groups=mesh['dp'=16,'ctx'=8] {'dp'}, dimensions={0} | all-to-all | bytes 1572864 | tf_op jit(solution)/shard_map/all_to_all | solution.py:307
  131.5 0.7 reduce_sum.32
  132.2 0.0 all-gather.6.cloned.1.call-update
  132.2 0.0 copy-done.2
  132.2 31.6 %all_to_all.16.refs_0_ = bf16[8,256,512]{2,1,0:T(8,128)(2,1)} all-to-all(bf16[8,256,512]{2,1,0:T(8,128)(2,1)S(1)} %bitcast.25), channel_id=1, replica_groups=mesh['dp'=16,'ctx'=8] {'ctx'}, dimensions={0} | all-to-all | bytes 4194304 | tf_op jit(solution)/shard_map/all_to_all | solution.py:320
  163.8 7.9 %finish.1 = (bf16[256,1024]{1,0:T(8,128)(2,1)}, bf16[256,1024]{1,0:T(8,128)(2,1)}) custom-call(bf16[8,256,512]{2,1,0:T(8,128)(2,1)} %all_to_all.16.refs_0_, bf16[1024,3072]{1,0:T(8,128)(2,1)} %refs_1_.1, bf16[256,1024]{1,0:T(8,128)(2,1)} %bitcast.22, bf16[256,1024]{1,0:T(8,128)(2,1)} %bitcast.23), custom_call_target="tpu_custom_call" | custom-call | tf_op jit(solution)/shard_map/finish/pallas_call | solution.py:322
  171.8 28.5 %all-gather.6.cloned.1.call-done = bf16[8192,384]{1,0:T(8,128)(2,1)} async-done(((bf16[64,384]{1,0:T(8,128)(2,1)}), bf16[8192,384]{1,0:T(8,128)(2,1)}) %all-gather.6.cloned.1.call-update) | async-done | bytes 6291472 | tf_op jit(solution)/shard_map/all_gather | solution.py:309
  200.3 12.3 %join.1 = f32[1024,3072]{1,0:T(8,128)} custom-call(bf16[128,64,384]{2,1,0:T(8,128)(2,1)} %bitcast.17), custom_call_target="tpu_custom_call" | custom-call | tf_op jit(solution)/shard_map/join/pallas_call | solution.py:310
Async XLA Ops:
  7.2 2.7 %copy-start.1 = (bf16[1,256,1024]{2,1,0:T(8,128)(2,1)S(1)}, bf16[1,256,1024]{2,1,0:T(8,128)(2,1)}, u32[]{:S(2)}) copy-start(bf16[1,256,1024]{2,1,0:T(8,128)(2,1)} %param.5) | copy-start | bytes 1572868
  7.2 40.2 %all-gather.4.cloned.1.call-start = ((), (), s32[]{:S(2)}) async-start(), calls=%async_computation.3 | async-start | bytes 5013504 | tf_op jit(solution)/shard_map/all_gather | solution.py:229
  10.9 39.8 %all-to-all-start = ((bf16[8,256,128]{2,1,0:T(8,128)(2,1)}), bf16[8,256,128]{2,1,0:T(8,128)(2,1)S(1)}, u32[]{:S(2)}, u32[]{:S(2)}) async-start(bf16[8,256,128]{2,1,0:T(8,128)(2,1)} %bitcast.16), calls=%async_computation | async-start | bytes 1048576 | tf_op jit(solution)/shard_map/all_to_all | solution.py:230
  17.7 182.6 %all-gather.6.cloned.1.call-start = ((), (), s32[]{:S(2)}) async-start(), calls=%async_computation.4 | async-start | bytes 6340608 | tf_op jit(solution)/shard_map/all_gather | solution.py:309
  50.7 0.8 copy-start
  106.1 26.1 %copy-start.2 = (bf16[2048,512]{1,0:T(8,128)(2,1)S(1)}, bf16[2048,512]{1,0:T(8,128)(2,1)}, u32[]{:S(2)}) copy-start(bf16[2048,512]{1,0:T(8,128)(2,1)} %get-tuple-element.17) | copy-start | bytes 6291460
Sparse Core Ops, SparseCore 0:
  10.3 37.0 all-gather.3
  132.3 67.9 all-gather.5

commit v2 on v1

v2 whole, which is shorter than its diff:
```python
import jax
import jax.numpy as jnp
from jax import lax
from jax.experimental import pallas as pl
from jax.experimental.pallas import tpu as pltpu
from jax.sharding import PartitionSpec as P

HEADS = 8
HEAD = 128
EPS = 1e-05
VMEM = 56 * 2**20
F32 = jnp.float32
BF16 = jnp.bfloat16

NN = (((1,), (0,)), ((), ()))
NT = (((1,), (1,)), ((), ()))
TN = (((0,), (0,)), ((), ()))


def dot(a, b, dims=NN):
    return lax.dot_general(a, b, dims, preferred_element_type=F32)


def normalize(value):
    centred = value - jnp.mean(value, axis=-1, keepdims=True)
    spread = jnp.mean(centred * centred, axis=-1, keepdims=True)
    return centred * lax.rsqrt(spread + EPS)


def silu_grad(value):
    half = 0.5 * value
    th = jnp.tanh(half)
    return 0.5 * (1.0 + th) * (1.0 + half * (1.0 - th))


def history_start(bounds, row):
    return jnp.where(row >= bounds[1], bounds[1], jnp.where(row >= bounds[0], bounds[0], 0))


def proj_kernel(order_ref, x_ref, w_ref, *refs):
    normed_ref, pre_ref, act_ref = refs[-3:]
    normed = normalize(x_ref[0].astype(F32)).astype(BF16)
    normed_ref[...] = normed
    pre = dot(normed, w_ref[...])
    pre_ref[...] = pre
    half = 0.5 * pre
    act_ref[...] = (half * (1.0 + jnp.tanh(half))).astype(BF16)


def fwd_kernel(rows, scale, place_ref, bounds_ref, act_ref, cot_ref, att_ref, stat_ref):
    step = pl.program_id(0)
    bounds = (bounds_ref[0], bounds_ref[1])
    here = pl.ds(pl.multiple_of(step * rows, rows), rows)
    query = act_ref[here, pl.ds(0, HEAD)]
    wide = 2 * rows
    end = (step + 1) * rows
    row = step * rows + lax.broadcasted_iota(jnp.int32, (rows, 1), 0)
    first = history_start(bounds, row)

    def inner(p, total):
        col0 = pl.multiple_of(jnp.maximum(end - (p + 1) * wide, 0), rows)
        there = pl.ds(col0, wide)
        keys = act_ref[there, pl.ds(HEAD, HEAD)]
        values = act_ref[there, pl.ds(2 * HEAD, HEAD)]
        t = dot(query, keys, NT) * (0.5 * scale)
        col = col0 + lax.broadcasted_iota(jnp.int32, (1, wide), 1)
        last = jnp.minimum(row, end - p * wide - 1)
        mask = (col <= last) & (col >= first)
        weights = jnp.where(mask, t * (1.0 + jnp.tanh(t)), 0.0).astype(BF16)
        return total + dot(weights, values)

    count = (end - history_start(bounds, step * rows) + wide - 1) // wide
    att = lax.fori_loop(0, count, inner, jnp.zeros((rows, HEAD), F32)) * (1.0 / 1024)
    att_t = att.T
    att_ref[...] = att_t
    cot_t = cot_ref[0].astype(F32).T
    mean = jnp.mean(att_t, axis=0, keepdims=True)
    centred = att_t - mean
    stat_ref[...] = jnp.concatenate(
        [
            mean,
            jnp.sum(centred * centred, axis=0, keepdims=True),
            jnp.sum(cot_t * centred, axis=0, keepdims=True),
            jnp.sum(cot_t, axis=0, keepdims=True),
        ],
        axis=0,
    )


def bwd_kernel(rows, scale, inv_root, place_ref, bounds_ref, act_ref, att_ref, cot_ref, stat0_ref,
               stat1_ref, stat2_ref, stat3_ref, normed_ref, pre_ref, out_ref, gw_ref, n_s, dq_s, dk_s,
               dv_s, gw_s):
    step = pl.program_id(0)
    steps = pl.num_programs(0) // 2
    bounds = (bounds_ref[0], bounds_ref[1])
    width = HEADS * HEAD

    @pl.when(step < steps)
    def _():
        stats = [ref[...] for ref in (stat0_ref, stat1_ref, stat2_ref, stat3_ref)]
        means, second, cross, sums = (
            jnp.concatenate([s[r + i : r + i + 1] for s in stats for r in (0, 4)], axis=0)
            for i in range(4)
        )
        mean = jnp.mean(means, axis=0, keepdims=True)
        shift = means - mean
        var = jnp.sum(second + HEAD * shift * shift, axis=0, keepdims=True) * (1.0 / width)
        factor = lax.rsqrt(var + EPS)
        mean_cot = jnp.sum(sums, axis=0, keepdims=True) * (1.0 / width)
        inner_mean = factor * jnp.sum(cross + shift * sums, axis=0, keepdims=True) * (1.0 / width)
        n_t = (att_ref[...] - mean) * factor
        cot_t = cot_ref[0].astype(F32).T
        ga_t = factor * (cot_t - mean_cot - n_t * inner_mean)
        here = pl.ds(pl.multiple_of(step * rows, rows), rows)
        n_s[here, :] = n_t.T.astype(BF16)
        grad_att = ga_t.T.astype(BF16)
        ga_tb = ga_t.astype(BF16)
        query = act_ref[here, pl.ds(0, HEAD)]
        query_t = query.astype(F32).T.astype(BF16)
        row = step * rows + lax.broadcasted_iota(jnp.int32, (rows, 1), 0)
        first = history_start(bounds, row)
        dk_s[step] = jnp.zeros((HEAD, rows), F32)
        dv_s[step] = jnp.zeros((HEAD, rows), F32)

        def inner(j, total):
            there = pl.ds(pl.multiple_of(j * rows, rows), rows)
            keys = act_ref[there, pl.ds(HEAD, HEAD)]
            values = act_ref[there, pl.ds(2 * HEAD, HEAD)]
            t = dot(query, keys, NT) * (0.5 * scale)
            prod = dot(grad_att, values, NT)
            col = j * rows + lax.broadcasted_iota(jnp.int32, (1, rows), 1)
            mask = (col <= row) & (col >= first)
            th = jnp.tanh(t)
            up = 1.0 + th
            weights = jnp.where(mask, t * up, 0.0).astype(BF16)
            grads = jnp.where(mask, prod * (up * (1.0 + t * (1.0 - th))), 0.0).astype(BF16)
            dv_s[j] += dot(ga_tb, weights)
            dk_s[j] += dot(query_t, grads)
            return total + dot(grads, keys)

        dq_s[here, :] = lax.fori_loop(
            history_start(bounds, step * rows) // rows, step + 1, inner, jnp.zeros((rows, HEAD), F32)
        )

    @pl.when(step >= steps)
    def _():
        block = step - steps
        here = pl.ds(pl.multiple_of(block * rows, rows), rows)
        slope = silu_grad(pre_ref[...])
        inv = 1.0 / 1024
        gpre = jnp.concatenate(
            [
                dq_s[here, :] * (0.5 * inv * scale),
                dk_s[block].T * (0.5 * inv * scale),
                dv_s[block].T * inv,
            ],
            axis=1,
        )
        gpre = (gpre * slope).astype(BF16)
        out_ref[:, pl.ds(0, HEAD)] = n_s[here, :]
        out_ref[:, pl.ds(HEAD, 3 * HEAD)] = gpre
        term = dot(normed_ref[...], gpre, TN)

        @pl.when(block == 0)
        def _():
            gw_s[...] = term

        @pl.when(block > 0)
        def _():
            gw_s[...] += term

        @pl.when(block == steps - 1)
        def _():
            gw_ref[...] = (gw_s[...] * inv_root).astype(BF16)


def out_kernel(rows, heads_ref, got0_ref, got1_ref, got2_ref, got3_ref, w_ref, x_ref, cot_ref,
               out_ref, gtok_ref, g_s, acc_s):
    step = pl.program_id(0)
    width = HEADS * HEAD
    part = w_ref.shape[0]

    @pl.when(step == 0)
    def _():
        for s, got_ref in enumerate((got0_ref, got1_ref, got2_ref, got3_ref)):
            for j in range(2):
                col = pl.multiple_of(heads_ref[2 * s + j] * HEAD, HEAD)
                out_ref[:, pl.ds(col, HEAD)] = (
                    x_ref[:, pl.ds(col, HEAD)].astype(F32) + got_ref[j, :, pl.ds(0, HEAD)].astype(F32)
                ).astype(BF16)
                for t in range(3):
                    g_s[:, pl.ds(t * width + col, HEAD)] = got_ref[j, :, pl.ds((t + 1) * HEAD, HEAD)]

    acc_s[step] = dot(g_s[...], w_ref[...], NT)

    @pl.when(step == pl.num_programs(0) - 1)
    def _():
        x = x_ref[...].astype(F32)
        centred = x - jnp.mean(x, axis=-1, keepdims=True)
        factor = lax.rsqrt(jnp.mean(centred * centred, axis=-1, keepdims=True) + EPS)
        normal = centred * factor
        grad = jnp.concatenate([acc_s[i] for i in range(width // part)], axis=1)
        back = factor * (
            grad
            - jnp.mean(grad, axis=-1, keepdims=True)
            - normal * jnp.mean(grad * normal, axis=-1, keepdims=True)
        )
        gtok_ref[...] = (cot_ref[...].astype(F32) + back).astype(BF16)


def join_kernel(piece, where_ref, *refs):
    same, other = refs[:4], refs[4:8]
    out_ref, buf, sem = refs[8:]
    step = pl.program_id(0)

    def fetch(q, wait):
        for side, group in enumerate((same, other)):
            rel = lax.rem(q - where_ref[side] + 4, 4)
            slot = lax.rem(q, 2)
            for a, ref in enumerate(group):

                @pl.when(rel == a)
                def _():
                    copy = pltpu.make_async_copy(ref, buf.at[slot, side], sem.at[slot, side])
                    copy.wait() if wait else copy.start()

    @pl.when(step == 0)
    def _():
        fetch(step, False)

    @pl.when(step + 1 < pl.num_programs(0))
    def _():
        fetch(step + 1, False)

    fetch(step, True)
    slot = lax.rem(step, 2)
    for side in range(2):
        for s in range(4):
            head = where_ref[2 + 4 * side + s]
            for t in range(3):
                col = pl.multiple_of((t * HEADS + head) * HEAD, HEAD)
                out_ref[:, pl.ds(col, HEAD)] = buf[slot, side, s, :, pl.ds(t * HEAD, HEAD)].astype(F32)


def params(n):
    return pltpu.CompilerParams(dimension_semantics=("arbitrary",) * n, vmem_limit_bytes=VMEM)


SIDE = 4


def ring(axis, step):
    pairs = []
    for place in range(2 * SIDE**3):
        core = place % 2
        at = [place // (2 * SIDE * SIDE), place // (2 * SIDE) % SIDE, place // 2 % SIDE]
        at[axis(core)] = (at[axis(core)] + step) % SIDE
        pairs.append((place, ((at[0] * SIDE + at[1]) * SIDE + at[2]) * 2 + core))
    return pairs


def along(axis):
    return lambda value, step: lax.ppermute(value, ("dp", "ctx"), ring(axis, step))


def along_z(value, step):
    return lax.ppermute(value, "ctx", [(c, (c + 2 * step) % 8) for c in range(8)])


def swap(value):
    return lax.ppermute(value, "ctx", [(c, c ^ 1) for c in range(8)])


def to_head(chunks, core, z):
    pairs = chunks.reshape((SIDE, 2) + chunks.shape[1:])
    pick = lambda a, i, dim: lax.dynamic_index_in_dim(a, i, dim, keepdims=False)
    mine = pick(pairs, core, 1)
    theirs = swap(pick(pairs, 1 - core, 1))
    send = lambda d: jnp.stack([pick(mine, (z + d) % SIDE, 0), pick(theirs, (z + d) % SIDE, 0)])
    far, after, before = (along_z(send(d), d) for d in (2, 1, -1))
    return send(0), after, before, far


def body(tokens, cotangent, proj_weight, segment):
    x_tok = tokens[0]
    grad_out = cotangent[0]
    seg_ids = segment[0]
    rows, width = x_tok.shape
    ctx_count = lax.axis_size("ctx")
    dp_count = lax.axis_size("dp")
    total = rows * ctx_count
    scale = 1.0 / HEAD**0.5
    inv_root = 1.0 / (dp_count * total) ** 0.5
    head = lax.axis_index("ctx")
    core, z = head % 2, head // 2
    x_at, y_at = lax.axis_index("dp") // SIDE, lax.axis_index("dp") % SIDE
    near = jnp.stack([head, (head + 6) % 8, (head + 2) % 8, (head + 4) % 8])
    order = jnp.stack([near, near ^ 1], axis=1).reshape(8).astype(jnp.int32)
    place = jnp.sum(
        jnp.where(order[:, None] == jnp.arange(8)[None, :], jnp.arange(8)[:, None], 0), axis=0
    ).astype(jnp.int32)

    before = along_z(x_tok, 1)
    after = along_z(x_tok, -1)
    partner = swap(x_tok)
    counts = jnp.stack([jnp.sum(seg_ids < 1), jnp.sum(seg_ids < 2)]).astype(F32)
    counts = jnp.broadcast_to(counts[:, None], (2, HEAD))
    counts = counts + swap(counts)
    counts = (counts + along_z(counts, 2)) + (along_z(counts, 1) + along_z(counts, -1))
    bounds = counts[:, 0].astype(jnp.int32)
    half = rows // 2
    far_low = along_z(before[:half], 1)
    far_high = along_z(after[half:], -1)
    w_head = jnp.concatenate(
        [lax.dynamic_slice_in_dim(proj_weight, t * width + head * HEAD, HEAD, 1) for t in range(3)],
        axis=1,
    )
    cot_chunks = grad_out.reshape(rows, HEADS, HEAD).transpose(1, 0, 2)
    cot_head = jnp.concatenate(to_head(cot_chunks, core, z), axis=0)

    def project(count, first, shards, earlier):
        return pl.pallas_call(
            proj_kernel,
            grid_spec=pltpu.PrefetchScalarGridSpec(
                num_scalar_prefetch=1,
                grid=(count,),
                in_specs=[
                    pl.BlockSpec((1, rows, width), lambda i, o: (i, 0, 0)),
                    pl.BlockSpec((width, 3 * HEAD), lambda i, o: (0, 0)),
                ]
                + [pl.BlockSpec(memory_space=pl.ANY)] * len(earlier),
                out_specs=[
                    pl.BlockSpec((rows, width), lambda i, o: (o[first + i], 0)),
                    pl.BlockSpec((rows, 3 * HEAD), lambda i, o: (o[first + i], 0)),
                    pl.BlockSpec((rows, 3 * HEAD), lambda i, o: (o[first + i], 0)),
                ],
            ),
            out_shape=[
                jax.ShapeDtypeStruct((total, width), BF16),
                jax.ShapeDtypeStruct((total, 3 * HEAD), F32),
                jax.ShapeDtypeStruct((total, 3 * HEAD), BF16),
            ],
            input_output_aliases={3 + i: i for i in range(len(earlier))},
            compiler_params=params(1),
            cost_estimate=pl.CostEstimate(
                flops=count * 2 * rows * width * 3 * HEAD,
                bytes_accessed=count * rows * width * 6,
                transcendentals=0,
            ),
            name="project",
        )(order, shards, w_head, *earlier)

    seen = project(
        6, 0, jnp.stack([x_tok, partner, before, swap(before), after, swap(after)]), ()
    )
    far = jnp.concatenate([far_low, far_high], axis=0)
    far_other = jnp.concatenate([swap(far_low), swap(far_high)], axis=0)
    normed, pre, act = project(2, 6, jnp.stack([far, far_other]), seen)

    att_t, stat = pl.pallas_call(
        lambda *refs: fwd_kernel(rows, scale, *refs),
        grid_spec=pltpu.PrefetchScalarGridSpec(
            num_scalar_prefetch=2,
            grid=(ctx_count,),
            in_specs=[
                pl.BlockSpec((total, 3 * HEAD), lambda i, p, b: (0, 0)),
                pl.BlockSpec((1, rows, HEAD), lambda i, p, b: (p[i], 0, 0)),
            ],
            out_specs=[
                pl.BlockSpec((HEAD, rows), lambda i, p, b: (0, i)),
                pl.BlockSpec((4, rows), lambda i, p, b: (0, i)),
            ],
        ),
        out_shape=[
            jax.ShapeDtypeStruct((HEAD, total), F32),
            jax.ShapeDtypeStruct((4, total), F32),
        ],
        compiler_params=params(1),
        name="attend",
    )(place, bounds, act, cot_head)

    pair = jnp.concatenate([stat, swap(stat)], axis=0)
    stats = (pair, along_z(pair, 2), along_z(pair, 1), along_z(pair, -1))

    late = lambda i: jnp.maximum(i - ctx_count, 0)
    early = lambda i: jnp.minimum(i, ctx_count - 1)
    back, gw = pl.pallas_call(
        lambda *refs: bwd_kernel(rows, scale, inv_root, *refs),
        grid_spec=pltpu.PrefetchScalarGridSpec(
            num_scalar_prefetch=2,
            grid=(2 * ctx_count,),
            in_specs=[
                pl.BlockSpec((total, 3 * HEAD), lambda i, p, b: (0, 0)),
                pl.BlockSpec((HEAD, rows), lambda i, p, b: (0, early(i))),
                pl.BlockSpec((1, rows, HEAD), lambda i, p, b: (p[early(i)], 0, 0)),
            ]
            + [pl.BlockSpec((8, rows), lambda i, p, b: (0, early(i)))] * 4
            + [
                pl.BlockSpec((rows, width), lambda i, p, b: (late(i), 0)),
                pl.BlockSpec((rows, 3 * HEAD), lambda i, p, b: (late(i), 0)),
            ],
            out_specs=[
                pl.BlockSpec((rows, 4 * HEAD), lambda i, p, b: (late(i), 0)),
                pl.BlockSpec((width, 3 * HEAD), lambda i, p, b: (0, 0)),
            ],
            scratch_shapes=[
                pltpu.VMEM((total, HEAD), BF16),
                pltpu.VMEM((total, HEAD), F32),
                pltpu.VMEM((ctx_count, HEAD, rows), F32),
                pltpu.VMEM((ctx_count, HEAD, rows), F32),
                pltpu.VMEM((width, 3 * HEAD), F32),
            ],
        ),
        out_shape=[
            jax.ShapeDtypeStruct((total, 4 * HEAD), BF16),
            jax.ShapeDtypeStruct((width, 3 * HEAD), BF16),
        ],
        compiler_params=params(1),
        name="attend_back",
    )(place, bounds, act, att_t, cot_head, *stats, normed, pre)

    first_way = along(lambda c: c)
    other_way = along(lambda c: 1 - c)
    piece = width // SIDE
    my_piece = jnp.where(core == 0, x_at, y_at)
    cut = lambda d: lax.dynamic_slice_in_dim(gw, (my_piece + d) % SIDE * piece, piece, 0)
    up = lambda v: v.astype(F32)
    terms = [first_way(cut(d), d) for d in (2, 1, -1)]
    summed = ((up(cut(0)) + up(terms[0])) + (up(terms[1]) + up(terms[2]))).astype(BF16)
    terms = [other_way(summed, d) for d in (2, 1, -1)]
    summed = ((up(summed) + up(terms[0])) + (up(terms[1]) + up(terms[2]))).astype(BF16)
    chips = jnp.stack([summed, along_z(summed, 1), along_z(summed, -1), along_z(summed, 2)])
    same = [chips, first_way(chips, -1), first_way(chips, 2), first_way(chips, 1)]
    other = [swap(v) for v in same]
    z_order = jnp.stack([z, (z + 3) % SIDE, (z + 1) % SIDE, (z + 2) % SIDE])
    where = jnp.concatenate(
        [
            jnp.stack([my_piece, jnp.where(core == 0, y_at, x_at)]),
            2 * z_order + core,
            2 * z_order + 1 - core,
        ]
    ).astype(jnp.int32)
    grad_weight = pl.pallas_call(
        lambda *refs: join_kernel(piece, *refs),
        grid_spec=pltpu.PrefetchScalarGridSpec(
            num_scalar_prefetch=1,
            grid=(SIDE,),
            in_specs=[pl.BlockSpec(memory_space=pl.ANY)] * 8,
            out_specs=pl.BlockSpec((piece, 3 * width), lambda i, w: (i, 0)),
            scratch_shapes=[
                pltpu.VMEM((2, 2, SIDE, piece, 3 * HEAD), BF16),
                pltpu.SemaphoreType.DMA((2, 2)),
            ],
        ),
        out_shape=jax.ShapeDtypeStruct((width, 3 * width), F32),
        compiler_params=params(1),
        name="join",
    )(where, *same, *other)

    mine = to_head(back.reshape(ctx_count, rows, 4 * HEAD), core, z)
    part = 256
    output, grad_tok = pl.pallas_call(
        lambda *refs: out_kernel(rows, *refs),
        grid_spec=pltpu.PrefetchScalarGridSpec(
            num_scalar_prefetch=1,
            grid=(width // part,),
            in_specs=[pl.BlockSpec((2, rows, 4 * HEAD), lambda i, o: (0, 0, 0))] * 4
            + [
                pl.BlockSpec((part, 3 * width), lambda i, o: (i, 0)),
                pl.BlockSpec((rows, width), lambda i, o: (0, 0)),
                pl.BlockSpec((rows, width), lambda i, o: (0, 0)),
            ],
            out_specs=[
                pl.BlockSpec((rows, width), lambda i, o: (0, 0)),
                pl.BlockSpec((rows, width), lambda i, o: (0, 0)),
            ],
            scratch_shapes=[
                pltpu.VMEM((rows, 3 * width), BF16),
                pltpu.VMEM((width // part, rows, part), F32),
            ],
        ),
        out_shape=[jax.ShapeDtypeStruct((rows, width), BF16)] * 2,
        compiler_params=params(1),
        cost_estimate=pl.CostEstimate(
            flops=2 * rows * width * 3 * width, bytes_accessed=10 * 2**20, transcendentals=0
        ),
        name="finish",
    )(order, *mine, proj_weight, x_tok, grad_out)
    return (output[None], grad_tok[None], grad_weight)


def solution(mesh):
    in_specs = (P("dp", "ctx", None), P("dp", "ctx", None), P(), P("dp", "ctx"))
    out_specs = (P("dp", "ctx", None), P("dp", "ctx", None), P())
    return jax.shard_map(body, mesh=mesh, in_specs=in_specs, out_specs=out_specs, check_vma=False)
```

time: 220 us -> 214 us (0.973)
  blocking collectives: 71.4 us -> 0 us
  starting transfers between devices: 6.85 us -> 63.3 us
  between operations: 14.1 us -> 1.19 us
  local copies, waits for them, and re-layouts: 3.72 us -> 14.3 us
  other arithmetic: 6.89 us -> 11.8 us
  waiting for transfers between devices: 56 us -> 59.3 us
  Pallas kernels: 60.4 us -> 63.1 us
    ppermute x0 -> x41, starting transfers between devices: none -> 63.3 us  [the longest x13 31 us: swap(): return lax.ppermute(value, 'ctx', [(c, c ^ 1) for c in range(8)])]
    ppermute x0 -> x41, waiting for transfers between devices: none -> 59.3 us  [the longest x19 43.5 us: along_z(): lax.ppermute(value, 'ctx', [(c, (c + 2 * step) % 8) for c in range(8)])]
    all_to_all x2 -> x0, blocking collectives: 57 us -> none  [the longest x1 31.6 us: body(): mine = lax.all_to_all(back.reshape(ctx_count, rows, 4 * HEAD), 'ctx', 0, 0)]
    all_gather x2 -> x0, waiting for transfers between devices: 56 us -> none  [the longest x1 28.5 us: body(): pieces = lax.all_gather(summed, ('dp', 'ctx'), axis=0, tiled=False)]
    all_gather x1 -> x0, blocking collectives: 14.5 us -> none  [body(): all_stat = lax.all_gather(stat, 'ctx', axis=0, tiled=True)]
    pallas_call x2 -> x4, Pallas kernels: 20.2 us -> 30 us  [the longest x2 12.6 us: project(): pl.pallas_call(proj_kernel, grid_spec=pltpu.PrefetchScalarGridSpec(num_sc...]
    pallas_call x1, Pallas kernels: 17.5 us -> 9.98 us  [body(): pl.pallas_call(lambda *refs: fwd_kernel(rows, scale, *refs), grid_spec=pl...]
    all_to_all x1 -> x0, starting transfers between devices: 6.81 us -> none  [body(): lax.all_to_all(grad_out.reshape(rows, HEADS, HEAD).transpose(1, 0, 2), 'c...]
  transfers between devices with their start and end apart: 3 -> 41, of which waited for: 2 -> 15; matrix products, arithmetic and copies ran while one was open for 3% -> 7% of each run, Pallas kernels for 4% -> 4%
where the time goes in v2:
time: 214 us; the launch traced here: 213 us
  starting transfers between devices  63.3 us (30%)
  Pallas kernels  63.1 us (29%)
  waiting for transfers between devices  59.3 us (28%)
  local copies, waits for them, and re-layouts  14.3 us (7%)
  other arithmetic  11.8 us (6%)
    ppermute x19, waiting for transfers between devices, along_z(): lax.ppermute(value, 'ctx', [(c, (c + 2 * step) % 8) for c in range(8)])  43.5 us
    ppermute x13, starting transfers between devices, swap(): return lax.ppermute(value, 'ctx', [(c, c ^ 1) for c in range(8)])  31 us
    pallas_call x1, Pallas kernels, body(): pl.pallas_call(lambda *refs: bwd_kernel(rows, scale, inv_root, *refs), gr...  23.1 us
    ppermute x19, starting transfers between devices, along_z(): lax.ppermute(value, 'ctx', [(c, (c + 2 * step) % 8) for c in range(8)])  20.5 us
    ppermute x9, waiting for transfers between devices, along(): lax.ppermute(value, ('dp', 'ctx'), ring(axis, step))  13.6 us
    pallas_call x2, Pallas kernels, project(): pl.pallas_call(proj_kernel, grid_spec=pltpu.PrefetchScalarGridSpec(num_sc...  12.6 us
    ppermute x9, starting transfers between devices, along(): lax.ppermute(value, ('dp', 'ctx'), ring(axis, step))  11.8 us
    pallas_call x1, Pallas kernels, body(): pl.pallas_call(lambda *refs: fwd_kernel(rows, scale, *refs), grid_spec=pl...  9.98 us
  transfers between devices with their start and end apart: 41, of which 15 were waited for; matrix products, arithmetic and copies ran while one was open for 7% of the time, Pallas kernels for 4%

profile of v2, /device:TPU:1, one launch (start us, length us, event | category | flops | bytes accessed | tf_op | source)
XLA Modules:
  0.0 213.1 jit_solution(5720261549216058178)
XLA Ops:
  0.6 1.4 fusion
  3.4 1.5 collective-permute-start
  4.9 3.9 %collective-permute-start.6 = (bf16[256,1024]{1,0:T(8,128)(2,1)}, bf16[256,1024]{1,0:T(8,128)(2,1)S(1)}, u32[]{:S(2)}, u32[]{:S(2)}) collective-permute-start(bf16[256,1024]{1,0:T(8,128)(2,1)} %bitcast.69), channel_id=1, source_target_pairs={{0,6},{1,7},{2,0},{3,1},{4,2},{5,3},{6,4},{7,5},{8,14},{9,15},{10,... | collective-permute-start | bytes 1572872 | tf_op jit(solution)/shard_map/ppermute | solution.py:267
  15.9 7.1 %collective-permute-done.3 = f32[2,128]{0,1:T(8,128)S(1)} collective-permute-done((f32[2,128]{0,1:T(8,128)S(1)}, f32[2,128]{0,1:T(8,128)S(1)}, u32[]{:S(2)}, u32[]{:S(2)}) %collective-permute-start.3) | collective-permute-done | bytes 1056 | tf_op jit(solution)/shard_map/ppermute | solution.py:267
  25.6 2.4 %collective-permute-start.15 = (bf16[2,256,128]{2,1,0:T(8,128)(2,1)S(1)}, bf16[2,256,128]{2,1,0:T(8,128)(2,1)S(1)}, u32[]{:S(2)}, u32[]{:S(2)}) collective-permute-start(bf16[2,256,128]{2,1,0:T(8,128)(2,1)S(1)} %pad_maximum_fusion.8), channel_id=1, source_target_pairs={{0,6},{1,7},{2,0},{3,1},{4,2},{5,3},{6,4},{7,5},{8,14},{9,15},{10,... | collective-permute-start | bytes 393224 | tf_op jit(solution)/shard_map/ppermute | solution.py:267
  28.1 12.6 %collective-permute-done.14 = bf16[2,256,128]{2,1,0:T(8,128)(2,1)S(1)} collective-permute-done((bf16[2,256,128]{2,1,0:T(8,128)(2,1)S(1)}, bf16[2,256,128]{2,1,0:T(8,128)(2,1)S(1)}, u32[]{:S(2)}, u32[]{:S(2)}) %collective-permute-start.14) | collective-permute-done | bytes 131104 | tf_op jit(solution)/shard_map/ppermute | solution.py:267
  42.7 3.3 %collective-permute-done.16 = bf16[2,256,128]{2,1,0:T(8,128)(2,1)S(1)} collective-permute-done((bf16[2,256,128]{2,1,0:T(8,128)(2,1)S(1)}, bf16[2,256,128]{2,1,0:T(8,128)(2,1)S(1)}, u32[]{:S(2)}, u32[]{:S(2)}) %collective-permute-start.16) | collective-permute-done | bytes 131104 | tf_op jit(solution)/shard_map/ppermute | solution.py:267
  46.0 4.0 %collective-permute-start.11 = (bf16[256,1024]{1,0:T(8,128)(2,1)S(1)}, bf16[256,1024]{1,0:T(8,128)(2,1)S(1)}, u32[]{:S(2)}, u32[]{:S(2)}) collective-permute-start(bf16[256,1024]{1,0:T(8,128)(2,1)S(1)} %collective-permute-done.4), channel_id=1, source_target_pairs={{0,1},{1,0},{2,3},{3,2},{4,5},{5,4},{6,7},{7,6},{8,9},{9,8},{10,11... | collective-permute-start | bytes 1572872 | tf_op jit(solution)/shard_map/ppermute | solution.py:271
  50.2 2.2 %collective-permute-start.9 = (bf16[128,1024]{1,0:T(8,128)(2,1)S(1)}, bf16[128,1024]{1,0:T(8,128)(2,1)S(1)}, u32[]{:S(2)}, u32[]{:S(2)}) collective-permute-start(bf16[128,1024]{1,0:T(8,128)(2,1)S(1)} %collective-permute-done.7), channel_id=1, source_target_pairs={{0,1},{1,0},{2,3},{3,2},{4,5},{5,4},{6,7},{7,6},{8,9},{9,8},{10,11... | collective-permute-start | bytes 786440 | tf_op jit(solution)/shard_map/ppermute | solution.py:271
  56.2 1.7 copy-done.13
  57.8 8.3 %project.2 = (bf16[2048,1024]{1,0:T(8,128)(2,1)}, f32[2048,384]{1,0:T(8,128)}, bf16[2048,384]{1,0:T(8,128)(2,1)}) custom-call(s32[8]{0:T(128)} %copy-done.17, bf16[6,256,1024]{2,1,0:T(8,128)(2,1)} %copy-done.13, bf16[1024,384]{1,0:T(8,128)(2,1)} %pad_maximum_fusion.1.w_ref), custom_call_target="tpu_custom_call" | custom-call | flops 1207959552 | bytes 9437184 | tf_op jit(solution)/shard_map/project/pallas_call | solution.py:322
  66.2 4.3 %project.3 = (bf16[2048,1024]{1,0:T(8,128)(2,1)}, f32[2048,384]{1,0:T(8,128)}, bf16[2048,384]{1,0:T(8,128)(2,1)}) custom-call(s32[8]{0:T(128)} %copy-done.17, bf16[2,256,1024]{2,1,0:T(8,128)(2,1)} %pad_maximum_fusion.x_ref, bf16[1024,384]{1,0:T(8,128)(2,1)} %pad_maximum_fusion.1.w_ref, ...), custom_call_target="tpu_custom_call", output_to_operand_aliasing={{0}: (3, {}), {1}: (4, {}), {2}: (5, {})} | custom-call | flops 402653184 | bytes 3145728 | tf_op jit(solution)/shard_map/project/pallas_call | solution.py:322
  70.4 10.0 %attend.1 = (f32[128,2048]{1,0:T(8,128)}, f32[4,2048]{1,0:T(4,128)}) custom-call(s32[8]{0:T(128)} %select_reduce_fusion.refs_0_, s32[2]{0:T(128)} %convert_bitcast_fusion.refs_1_, bf16[2048,384]{1,0:T(8,128)(2,1)} %get-tuple-element.18.refs_2_, bf16[8,256,128]{2,1,0:T(8,128)(2,1)} %copy-done.1), custom_call_target="tpu_custom_call" | custom-call | tf_op jit(solution)/shard_map/attend/pallas_call | solution.py:360
  84.7 1.6 collective-permute-start.20
  87.4 1.9 collective-permute-done.19.refs_7_
  89.9 23.1 %attend_back.1 = (bf16[2048,512]{1,0:T(8,128)(2,1)}, bf16[1024,384]{1,0:T(8,128)(2,1)}) custom-call(s32[8]{0:T(128)} %select_reduce_fusion.refs_0_, s32[2]{0:T(128)} %convert_bitcast_fusion.refs_1_, bf16[2048,384]{1,0:T(8,128)(2,1)} %get-tuple-element.18.refs_2_, f32[128,2048]{1,0:T(8,128)} %get-tuple-element.19.refs_3_, bf16[8,256,128]{2,1,0:T(8,128)(2,1)} %copy-done.1, ...), custom_call_target="tpu_custom_call" | custom-call | tf_op jit(solution)/shard_map/attend_back/pallas_call | solution.py:387
  113.0 2.1 constant_dynamic-slice_fusion.2
  115.1 4.1 %collective-permute-start.27 = (bf16[256,384]{1,0:T(8,128)(2,1)}, bf16[256,384]{1,0:T(8,128)(2,1)S(1)}, u32[]{:S(2)}, u32[]{:S(2)}) collective-permute-start(bf16[256,384]{1,0:T(8,128)(2,1)} %get-tuple-element.43), channel_id=1, source_target_pairs={{0,96},{1,25},{2,98},{3,27},{4,100},{5,29},{6,102},{7,31},{8,104},... | collective-permute-start | bytes 589832 | tf_op jit(solution)/shard_map/ppermute | solution.py:263
  120.4 2.3 %dynamic-slice_bitcast_fusion = bf16[4,256,512]{2,1,0:T(8,128)(2,1)} fusion(bf16[4,2,256,512]{3,2,1,0:T(8,128)(2,1)} %bitcast.78, s32[]{:T(128)S(6)} %select_n.185), kind=kLoop, calls=%fused_computation.1 | loop fusion | bytes 2097156 | tf_op jit(solution)/shard_map/jit(dynamic_index_in_dim)/squeeze | solution.py:276
  122.6 4.7 %collective-permute-start.21 = (bf16[4,256,512]{2,1,0:T(8,128)(2,1)}, bf16[4,256,512]{2,1,0:T(8,128)(2,1)S(1)}, u32[]{:S(2)}, u32[]{:S(2)}) collective-permute-start(bf16[4,256,512]{2,1,0:T(8,128)(2,1)} %dynamic-slice_bitcast_fusion), channel_id=1, source_target_pairs={{0,1},{1,0},{2,3},{3,2},{4,5},{5,4},{6,7},{7,6},{8,9},{9,8},{10,11... | collective-permute-start | bytes 3145736 | tf_op jit(solution)/shard_map/ppermute | solution.py:271
  128.6 3.7 %collective-permute-start.30 = (bf16[256,384]{1,0:T(8,128)(2,1)S(1)}, bf16[256,384]{1,0:T(8,128)(2,1)S(1)}, u32[]{:S(2)}, u32[]{:S(2)}) collective-permute-start(bf16[256,384]{1,0:T(8,128)(2,1)S(1)} %add_convert_fusion.1), channel_id=1, source_target_pairs={{0,24},{1,97},{2,26},{3,99},{4,28},{5,101},{6,30},{7,103},{8,0},{9... | collective-permute-start | bytes 589832 | tf_op jit(solution)/shard_map/ppermute | solution.py:263
  134.9 5.5 %collective-permute-done.29 = bf16[256,384]{1,0:T(8,128)(2,1)S(1)} collective-permute-done((bf16[256,384]{1,0:T(8,128)(2,1)S(1)}, bf16[256,384]{1,0:T(8,128)(2,1)S(1)}, u32[]{:S(2)}, u32[]{:S(2)}) %collective-permute-start.29) | collective-permute-done | bytes 196640 | tf_op jit(solution)/shard_map/ppermute | solution.py:263
  143.8 2.9 %collective-permute-done.33 = bf16[256,384]{1,0:T(8,128)(2,1)S(1)} collective-permute-done((bf16[256,384]{1,0:T(8,128)(2,1)S(1)}, bf16[256,384]{1,0:T(8,128)(2,1)S(1)}, u32[]{:S(2)}, u32[]{:S(2)}) %collective-permute-start.33) | collective-permute-done | bytes 196640 | tf_op jit(solution)/shard_map/ppermute | solution.py:267
  152.7 2.7 %collective-permute-start.23 = (bf16[2,256,512]{2,1,0:T(8,128)(2,1)}, bf16[2,256,512]{2,1,0:T(8,128)(2,1)S(1)}, u32[]{:S(2)}, u32[]{:S(2)}) collective-permute-start(bf16[2,256,512]{2,1,0:T(8,128)(2,1)} %pad_maximum_fusion.5), channel_id=1, source_target_pairs={{0,6},{1,7},{2,0},{3,1},{4,2},{5,3},{6,4},{7,5},{8,14},{9,15},{10,... | collective-permute-start | bytes 1572872 | tf_op jit(solution)/shard_map/ppermute | solution.py:267
  155.4 5.3 %collective-permute-done.34.refs_2_ = bf16[4,256,384]{2,1,0:T(8,128)(2,1)} collective-permute-done((bf16[4,256,384]{2,1,0:T(8,128)(2,1)S(1)}, bf16[4,256,384]{2,1,0:T(8,128)(2,1)}, u32[]{:S(2)}, u32[]{:S(2)}) %collective-permute-start.34) | collective-permute-done | bytes 786464 | tf_op jit(solution)/shard_map/ppermute | solution.py:263
  160.7 5.9 %collective-permute-start.37 = (bf16[4,256,384]{2,1,0:T(8,128)(2,1)S(1)}, bf16[4,256,384]{2,1,0:T(8,128)(2,1)S(1)}, u32[]{:S(2)}, u32[]{:S(2)}) collective-permute-start(bf16[4,256,384]{2,1,0:T(8,128)(2,1)S(1)} %pad_maximum_fusion.2.refs_1_), channel_id=1, source_target_pairs={{0,1},{1,0},{2,3},{3,2},{4,5},{5,4},{6,7},{7,6},{8,9},{9,8},{10,11... | collective-permute-start | bytes 2359304 | tf_op jit(solution)/shard_map/ppermute | solution.py:271
  166.6 2.8 %collective-permute-start.38 = (bf16[4,256,384]{2,1,0:T(8,128)(2,1)}, bf16[4,256,384]{2,1,0:T(8,128)(2,1)S(1)}, u32[]{:S(2)}, u32[]{:S(2)}) collective-permute-start(bf16[4,256,384]{2,1,0:T(8,128)(2,1)} %collective-permute-done.34.refs_2_), channel_id=1, source_target_pairs={{0,1},{1,0},{2,3},{3,2},{4,5},{5,4},{6,7},{7,6},{8,9},{9,8},{10,11... | collective-permute-start | bytes 2359304 | tf_op jit(solution)/shard_map/ppermute | solution.py:271
  169.4 1.4 collective-permute-done.36.refs_4_
  170.8 6.9 %collective-permute-start.39 = (bf16[4,256,384]{2,1,0:T(8,128)(2,1)}, bf16[4,256,384]{2,1,0:T(8,128)(2,1)S(1)}, u32[]{:S(2)}, u32[]{:S(2)}) collective-permute-start(bf16[4,256,384]{2,1,0:T(8,128)(2,1)} %collective-permute-done.35.refs_3_), channel_id=1, source_target_pairs={{0,1},{1,0},{2,3},{3,2},{4,5},{5,4},{6,7},{7,6},{8,9},{9,8},{10,11... | collective-permute-start | bytes 2359304 | tf_op jit(solution)/shard_map/ppermute | solution.py:271
  180.3 12.0 %collective-permute-done.24.refs_4_ = bf16[2,256,512]{2,1,0:T(8,128)(2,1)S(1)} collective-permute-done((bf16[2,256,512]{2,1,0:T(8,128)(2,1)S(1)}, bf16[2,256,512]{2,1,0:T(8,128)(2,1)S(1)}, u32[]{:S(2)}, u32[]{:S(2)}) %collective-permute-start.24) | collective-permute-done | bytes 524320 | tf_op jit(solution)/shard_map/ppermute | solution.py:267
  193.2 8.5 %finish.1 = (bf16[256,1024]{1,0:T(8,128)(2,1)}, bf16[256,1024]{1,0:T(8,128)(2,1)}) custom-call(s32[8]{0:T(128)} %copy-done.17, bf16[2,256,512]{2,1,0:T(8,128)(2,1)} %pad_maximum_fusion.3.refs_1_, bf16[2,256,512]{2,1,0:T(8,128)(2,1)} %collective-permute-done.22.refs_2_, bf16[2,256,512]{2,1,0:T(8,128)(2,1)} %copy-done.9, bf16[2,256,512]{2,1,0:T(8,128)(2,1)} %copy-done.10, ...), custom_call_target="tpu_custom_call" | custom-call | flops 1610612736 | bytes 10485760 | tf_op jit(solution)/shard_map/finish/pallas_call | solution.py:462
  204.1 8.9 %join.1 = f32[1024,3072]{1,0:T(8,128)} custom-call(s32[10]{0:T(128)} %pad_add_fusion.1.refs_0_, bf16[4,256,384]{2,1,0:T(8,128)(2,1)} %copy-done, bf16[4,256,384]{2,1,0:T(8,128)(2,1)} %collective-permute-done.34.refs_2_, bf16[4,256,384]{2,1,0:T(8,128)(2,1)} %collective-permute-done.35.refs_3_, bf16[4,256,384]{2,1,0:T(8,128)(2,1)} %collective-permute-done.36.refs_4_, ...), custom_call_target="tpu_custom_call" | custom-call | tf_op jit(solution)/shard_map/join/pallas_call | solution.py:443
  (143 shorter events, 43.0 us)
Async XLA Ops:
  3.4 10.4 %collective-permute-start = (f32[2,128]{0,1:T(8,128)S(1)}, f32[2,128]{0,1:T(8,128)S(1)}, u32[]{:S(2)}, u32[]{:S(2)}) collective-permute-start(f32[2,128]{0,1:T(8,128)S(1)} %broadcast_in_dim.28), channel_id=1, source_target_pairs={{0,1},{1,0},{2,3},{3,2},{4,5},{5,4},{6,7},{7,6},{8,9},{9,8},{10,11... | collective-permute-start | bytes 3080 | tf_op jit(solution)/shard_map/ppermute | solution.py:271
  4.9 36.0 %collective-permute-start.6 = (bf16[256,1024]{1,0:T(8,128)(2,1)}, bf16[256,1024]{1,0:T(8,128)(2,1)S(1)}, u32[]{:S(2)}, u32[]{:S(2)}) collective-permute-start(bf16[256,1024]{1,0:T(8,128)(2,1)} %bitcast.69), channel_id=1, source_target_pairs={{0,6},{1,7},{2,0},{3,1},{4,2},{5,3},{6,4},{7,5},{8,14},{9,15},{10,... | collective-permute-start | bytes 1572872 | tf_op jit(solution)/shard_map/ppermute | solution.py:267
  10.0 14.4 %collective-permute-start.13 = (bf16[4,256,128]{2,1,0:T(8,128)(2,1)S(1)}, bf16[4,256,128]{2,1,0:T(8,128)(2,1)S(1)}, u32[]{:S(2)}, u32[]{:S(2)}) collective-permute-start(bf16[4,256,128]{2,1,0:T(8,128)(2,1)S(1)} %dynamic-slice_bitcast_fusion.5), channel_id=1, source_target_pairs={{0,1},{1,0},{2,3},{3,2},{4,5},{5,4},{6,7},{7,6},{8,9},{9,8},{10,11... | collective-permute-start | bytes 786440 | tf_op jit(solution)/shard_map/ppermute | solution.py:271
  13.8 9.2 %collective-permute-start.3 = (f32[2,128]{0,1:T(8,128)S(1)}, f32[2,128]{0,1:T(8,128)S(1)}, u32[]{:S(2)}, u32[]{:S(2)}) collective-permute-start(f32[2,128]{0,1:T(8,128)S(1)} %broadcast_add_fusion), channel_id=1, source_target_pairs={{0,6},{1,7},{2,0},{3,1},{4,2},{5,3},{6,4},{7,5},{8,14},{9,15},{10,... | collective-permute-start | bytes 3080 | tf_op jit(solution)/shard_map/ppermute | solution.py:267
  14.0 9.0 %collective-permute-start.2 = (f32[2,128]{0,1:T(8,128)S(1)}, f32[2,128]{0,1:T(8,128)S(1)}, u32[]{:S(2)}, u32[]{:S(2)}) collective-permute-start(f32[2,128]{0,1:T(8,128)S(1)} %broadcast_add_fusion), channel_id=1, source_target_pairs={{0,2},{1,3},{2,4},{3,5},{4,6},{5,7},{6,0},{7,1},{8,10},{9,11},{10,... | collective-permute-start | bytes 3080 | tf_op jit(solution)/shard_map/ppermute | solution.py:267
  15.3 8.5 %collective-permute-start.1 = (f32[2,128]{0,1:T(8,128)S(1)}, f32[2,128]{0,1:T(8,128)S(1)}, u32[]{:S(2)}, u32[]{:S(2)}) collective-permute-start(f32[2,128]{0,1:T(8,128)S(1)} %broadcast_add_fusion), channel_id=1, source_target_pairs={{0,4},{1,5},{2,6},{3,7},{4,0},{5,1},{6,2},{7,3},{8,12},{9,13},{10,... | collective-permute-start | bytes 3080 | tf_op jit(solution)/shard_map/ppermute | solution.py:267
  23.0 19.0 %collective-permute-start.4 = (bf16[256,1024]{1,0:T(8,128)(2,1)S(1)}, bf16[256,1024]{1,0:T(8,128)(2,1)S(1)}, u32[]{:S(2)}, u32[]{:S(2)}) collective-permute-start(bf16[256,1024]{1,0:T(8,128)(2,1)S(1)} %bitcast.71), channel_id=1, source_target_pairs={{0,2},{1,3},{2,4},{3,5},{4,6},{5,7},{6,0},{7,1},{8,10},{9,11},{10,... | collective-permute-start | bytes 1572872 | tf_op jit(solution)/shard_map/ppermute | solution.py:267
  23.0 27.2 %collective-permute-start.10 = (bf16[256,1024]{1,0:T(8,128)(2,1)S(1)}, bf16[256,1024]{1,0:T(8,128)(2,1)S(1)}, u32[]{:S(2)}, u32[]{:S(2)}) collective-permute-start(bf16[256,1024]{1,0:T(8,128)(2,1)S(1)} %bitcast.72), channel_id=1, source_target_pairs={{0,1},{1,0},{2,3},{3,2},{4,5},{5,4},{6,7},{7,6},{8,9},{9,8},{10,11... | collective-permute-start | bytes 1572872 | tf_op jit(solution)/shard_map/ppermute | solution.py:271
  24.5 16.2 %collective-permute-start.14 = (bf16[2,256,128]{2,1,0:T(8,128)(2,1)S(1)}, bf16[2,256,128]{2,1,0:T(8,128)(2,1)S(1)}, u32[]{:S(2)}, u32[]{:S(2)}) collective-permute-start(bf16[2,256,128]{2,1,0:T(8,128)(2,1)S(1)} %pad_maximum_fusion.7), channel_id=1, source_target_pairs={{0,2},{1,3},{2,4},{3,5},{4,6},{5,7},{6,0},{7,1},{8,10},{9,11},{10,... | collective-permute-start | bytes 393224 | tf_op jit(solution)/shard_map/ppermute | solution.py:267
  25.6 15.2 %collective-permute-start.15 = (bf16[2,256,128]{2,1,0:T(8,128)(2,1)S(1)}, bf16[2,256,128]{2,1,0:T(8,128)(2,1)S(1)}, u32[]{:S(2)}, u32[]{:S(2)}) collective-permute-start(bf16[2,256,128]{2,1,0:T(8,128)(2,1)S(1)} %pad_maximum_fusion.8), channel_id=1, source_target_pairs={{0,6},{1,7},{2,0},{3,1},{4,2},{5,3},{6,4},{7,5},{8,14},{9,15},{10,... | collective-permute-start | bytes 393224 | tf_op jit(solution)/shard_map/ppermute | solution.py:267
  40.9 9.4 %collective-permute-start.7 = (bf16[128,1024]{1,0:T(8,128)(2,1)S(1)}, bf16[128,1024]{1,0:T(8,128)(2,1)S(1)}, u32[]{:S(2)}, u32[]{:S(2)}) collective-permute-start(bf16[128,1024]{1,0:T(8,128)(2,1)S(1)} %slice.17), channel_id=1, source_target_pairs={{0,6},{1,7},{2,0},{3,1},{4,2},{5,3},{6,4},{7,5},{8,14},{9,15},{10,... | collective-permute-start | bytes 786440 | tf_op jit(solution)/shard_map/ppermute | solution.py:267
  42.0 10.5 %collective-permute-start.5 = (bf16[128,1024]{1,0:T(8,128)(2,1)S(1)}, bf16[128,1024]{1,0:T(8,128)(2,1)S(1)}, u32[]{:S(2)}, u32[]{:S(2)}) collective-permute-start(bf16[128,1024]{1,0:T(8,128)(2,1)S(1)} %slice.16), channel_id=1, source_target_pairs={{0,2},{1,3},{2,4},{3,5},{4,6},{5,7},{6,0},{7,1},{8,10},{9,11},{10,... | collective-permute-start | bytes 786440 | tf_op jit(solution)/shard_map/ppermute | solution.py:267
  46.0 10.0 %collective-permute-start.11 = (bf16[256,1024]{1,0:T(8,128)(2,1)S(1)}, bf16[256,1024]{1,0:T(8,128)(2,1)S(1)}, u32[]{:S(2)}, u32[]{:S(2)}) collective-permute-start(bf16[256,1024]{1,0:T(8,128)(2,1)S(1)} %collective-permute-done.4), channel_id=1, source_target_pairs={{0,1},{1,0},{2,3},{3,2},{4,5},{5,4},{6,7},{7,6},{8,9},{9,8},{10,11... | collective-permute-start | bytes 1572872 | tf_op jit(solution)/shard_map/ppermute | solution.py:271
  115.1 12.2 %collective-permute-start.27 = (bf16[256,384]{1,0:T(8,128)(2,1)}, bf16[256,384]{1,0:T(8,128)(2,1)S(1)}, u32[]{:S(2)}, u32[]{:S(2)}) collective-permute-start(bf16[256,384]{1,0:T(8,128)(2,1)} %get-tuple-element.43), channel_id=1, source_target_pairs={{0,96},{1,25},{2,98},{3,27},{4,100},{5,29},{6,102},{7,31},{8,104},... | collective-permute-start | bytes 589832 | tf_op jit(solution)/shard_map/ppermute | solution.py:263
  119.2 8.2 %collective-permute-start.26 = (bf16[256,384]{1,0:T(8,128)(2,1)}, bf16[256,384]{1,0:T(8,128)(2,1)}, u32[]{:S(2)}, u32[]{:S(2)}) collective-permute-start(bf16[256,384]{1,0:T(8,128)(2,1)} %get-tuple-element.44), channel_id=1, source_target_pairs={{0,32},{1,9},{2,34},{3,11},{4,36},{5,13},{6,38},{7,15},{8,40},{9,1... | collective-permute-start | bytes 589832 | tf_op jit(solution)/shard_map/ppermute | solution.py:263
  119.2 8.2 %collective-permute-start.25 = (bf16[256,384]{1,0:T(8,128)(2,1)S(1)}, bf16[256,384]{1,0:T(8,128)(2,1)}, u32[]{:S(2)}, u32[]{:S(2)}) collective-permute-start(bf16[256,384]{1,0:T(8,128)(2,1)S(1)} %get-tuple-element.42), channel_id=1, source_target_pairs={{0,64},{1,17},{2,66},{3,19},{4,68},{5,21},{6,70},{7,23},{8,72},{9,... | collective-permute-start | bytes 589832 | tf_op jit(solution)/shard_map/ppermute | solution.py:263
  122.6 28.3 %collective-permute-start.21 = (bf16[4,256,512]{2,1,0:T(8,128)(2,1)}, bf16[4,256,512]{2,1,0:T(8,128)(2,1)S(1)}, u32[]{:S(2)}, u32[]{:S(2)}) collective-permute-start(bf16[4,256,512]{2,1,0:T(8,128)(2,1)} %dynamic-slice_bitcast_fusion), channel_id=1, source_target_pairs={{0,1},{1,0},{2,3},{3,2},{4,5},{5,4},{6,7},{7,6},{8,9},{9,8},{10,11... | collective-permute-start | bytes 3145736 | tf_op jit(solution)/shard_map/ppermute | solution.py:271
  128.6 6.4 %collective-permute-start.30 = (bf16[256,384]{1,0:T(8,128)(2,1)S(1)}, bf16[256,384]{1,0:T(8,128)(2,1)S(1)}, u32[]{:S(2)}, u32[]{:S(2)}) collective-permute-start(bf16[256,384]{1,0:T(8,128)(2,1)S(1)} %add_convert_fusion.1), channel_id=1, source_target_pairs={{0,24},{1,97},{2,26},{3,99},{4,28},{5,101},{6,30},{7,103},{8,0},{9... | collective-permute-start | bytes 589832 | tf_op jit(solution)/shard_map/ppermute | solution.py:263
  132.3 8.1 %collective-permute-start.29 = (bf16[256,384]{1,0:T(8,128)(2,1)S(1)}, bf16[256,384]{1,0:T(8,128)(2,1)S(1)}, u32[]{:S(2)}, u32[]{:S(2)}) collective-permute-start(bf16[256,384]{1,0:T(8,128)(2,1)S(1)} %add_convert_fusion.1), channel_id=1, source_target_pairs={{0,8},{1,33},{2,10},{3,35},{4,12},{5,37},{6,14},{7,39},{8,16},{9,4... | collective-permute-start | bytes 589832 | tf_op jit(solution)/shard_map/ppermute | solution.py:263
  132.3 8.1 %collective-permute-start.28 = (bf16[256,384]{1,0:T(8,128)(2,1)S(1)}, bf16[256,384]{1,0:T(8,128)(2,1)S(1)}, u32[]{:S(2)}, u32[]{:S(2)}) collective-permute-start(bf16[256,384]{1,0:T(8,128)(2,1)S(1)} %add_convert_fusion.1), channel_id=1, source_target_pairs={{0,16},{1,65},{2,18},{3,67},{4,20},{5,69},{6,22},{7,71},{8,24},{9,... | collective-permute-start | bytes 589832 | tf_op jit(solution)/shard_map/ppermute | solution.py:263
  141.6 6.5 %collective-permute-start.32 = (bf16[256,384]{1,0:T(8,128)(2,1)S(1)}, bf16[256,384]{1,0:T(8,128)(2,1)S(1)}, u32[]{:S(2)}, u32[]{:S(2)}) collective-permute-start(bf16[256,384]{1,0:T(8,128)(2,1)S(1)} %add_convert_fusion), channel_id=1, source_target_pairs={{0,6},{1,7},{2,0},{3,1},{4,2},{5,3},{6,4},{7,5},{8,14},{9,15},{10,... | collective-permute-start | bytes 589832 | tf_op jit(solution)/shard_map/ppermute | solution.py:267
  142.6 6.7 %collective-permute-start.31 = (bf16[256,384]{1,0:T(8,128)(2,1)S(1)}, bf16[256,384]{1,0:T(8,128)(2,1)S(1)}, u32[]{:S(2)}, u32[]{:S(2)}) collective-permute-start(bf16[256,384]{1,0:T(8,128)(2,1)S(1)} %add_convert_fusion), channel_id=1, source_target_pairs={{0,2},{1,3},{2,4},{3,5},{4,6},{5,7},{6,0},{7,1},{8,10},{9,11},{10,... | collective-permute-start | bytes 589832 | tf_op jit(solution)/shard_map/ppermute | solution.py:267
  149.4 11.3 %collective-permute-start.34 = (bf16[4,256,384]{2,1,0:T(8,128)(2,1)S(1)}, bf16[4,256,384]{2,1,0:T(8,128)(2,1)}, u32[]{:S(2)}, u32[]{:S(2)}) collective-permute-start(bf16[4,256,384]{2,1,0:T(8,128)(2,1)S(1)} %pad_maximum_fusion.2.refs_1_), channel_id=1, source_target_pairs={{0,96},{1,25},{2,98},{3,27},{4,100},{5,29},{6,102},{7,31},{8,104},... | collective-permute-start | bytes 2359304 | tf_op jit(solution)/shard_map/ppermute | solution.py:263
  149.7 17.0 %collective-permute-start.35 = (bf16[4,256,384]{2,1,0:T(8,128)(2,1)S(1)}, bf16[4,256,384]{2,1,0:T(8,128)(2,1)}, u32[]{:S(2)}, u32[]{:S(2)}) collective-permute-start(bf16[4,256,384]{2,1,0:T(8,128)(2,1)S(1)} %pad_maximum_fusion.2.refs_1_), channel_id=1, source_target_pairs={{0,64},{1,17},{2,66},{3,19},{4,68},{5,21},{6,70},{7,23},{8,72},{9,... | collective-permute-start | bytes 2359304 | tf_op jit(solution)/shard_map/ppermute | solution.py:263
  150.1 20.7 %collective-permute-start.36 = (bf16[4,256,384]{2,1,0:T(8,128)(2,1)S(1)}, bf16[4,256,384]{2,1,0:T(8,128)(2,1)}, u32[]{:S(2)}, u32[]{:S(2)}) collective-permute-start(bf16[4,256,384]{2,1,0:T(8,128)(2,1)S(1)} %pad_maximum_fusion.2.refs_1_), channel_id=1, source_target_pairs={{0,32},{1,9},{2,34},{3,11},{4,36},{5,13},{6,38},{7,15},{8,40},{9,1... | collective-permute-start | bytes 2359304 | tf_op jit(solution)/shard_map/ppermute | solution.py:263
  151.9 25.9 %collective-permute-start.22 = (bf16[2,256,512]{2,1,0:T(8,128)(2,1)}, bf16[2,256,512]{2,1,0:T(8,128)(2,1)}, u32[]{:S(2)}, u32[]{:S(2)}) collective-permute-start(bf16[2,256,512]{2,1,0:T(8,128)(2,1)} %pad_maximum_fusion.4), channel_id=1, source_target_pairs={{0,2},{1,3},{2,4},{3,5},{4,6},{5,7},{6,0},{7,1},{8,10},{9,11},{10,... | collective-permute-start | bytes 1572872 | tf_op jit(solution)/shard_map/ppermute | solution.py:267
  152.7 25.1 %collective-permute-start.23 = (bf16[2,256,512]{2,1,0:T(8,128)(2,1)}, bf16[2,256,512]{2,1,0:T(8,128)(2,1)S(1)}, u32[]{:S(2)}, u32[]{:S(2)}) collective-permute-start(bf16[2,256,512]{2,1,0:T(8,128)(2,1)} %pad_maximum_fusion.5), channel_id=1, source_target_pairs={{0,6},{1,7},{2,0},{3,1},{4,2},{5,3},{6,4},{7,5},{8,14},{9,15},{10,... | collective-permute-start | bytes 1572872 | tf_op jit(solution)/shard_map/ppermute | solution.py:267
  160.7 41.0 %collective-permute-start.37 = (bf16[4,256,384]{2,1,0:T(8,128)(2,1)S(1)}, bf16[4,256,384]{2,1,0:T(8,128)(2,1)S(1)}, u32[]{:S(2)}, u32[]{:S(2)}) collective-permute-start(bf16[4,256,384]{2,1,0:T(8,128)(2,1)S(1)} %pad_maximum_fusion.2.refs_1_), channel_id=1, source_target_pairs={{0,1},{1,0},{2,3},{3,2},{4,5},{5,4},{6,7},{7,6},{8,9},{9,8},{10,11... | collective-permute-start | bytes 2359304 | tf_op jit(solution)/shard_map/ppermute | solution.py:271
  166.6 35.1 %collective-permute-start.38 = (bf16[4,256,384]{2,1,0:T(8,128)(2,1)}, bf16[4,256,384]{2,1,0:T(8,128)(2,1)S(1)}, u32[]{:S(2)}, u32[]{:S(2)}) collective-permute-start(bf16[4,256,384]{2,1,0:T(8,128)(2,1)} %collective-permute-done.34.refs_2_), channel_id=1, source_target_pairs={{0,1},{1,0},{2,3},{3,2},{4,5},{5,4},{6,7},{7,6},{8,9},{9,8},{10,11... | collective-permute-start | bytes 2359304 | tf_op jit(solution)/shard_map/ppermute | solution.py:271
  170.8 30.9 %collective-permute-start.39 = (bf16[4,256,384]{2,1,0:T(8,128)(2,1)}, bf16[4,256,384]{2,1,0:T(8,128)(2,1)S(1)}, u32[]{:S(2)}, u32[]{:S(2)}) collective-permute-start(bf16[4,256,384]{2,1,0:T(8,128)(2,1)} %collective-permute-done.35.refs_3_), channel_id=1, source_target_pairs={{0,1},{1,0},{2,3},{3,2},{4,5},{5,4},{6,7},{7,6},{8,9},{9,8},{10,11... | collective-permute-start | bytes 2359304 | tf_op jit(solution)/shard_map/ppermute | solution.py:271
  177.7 24.1 %collective-permute-start.40 = (bf16[4,256,384]{2,1,0:T(8,128)(2,1)}, bf16[4,256,384]{2,1,0:T(8,128)(2,1)S(1)}, u32[]{:S(2)}, u32[]{:S(2)}) collective-permute-start(bf16[4,256,384]{2,1,0:T(8,128)(2,1)} %collective-permute-done.36.refs_4_), channel_id=1, source_target_pairs={{0,1},{1,0},{2,3},{3,2},{4,5},{5,4},{6,7},{7,6},{8,9},{9,8},{10,11... | collective-permute-start | bytes 2359304 | tf_op jit(solution)/shard_map/ppermute | solution.py:271
  177.8 14.6 %collective-permute-start.24 = (bf16[2,256,512]{2,1,0:T(8,128)(2,1)S(1)}, bf16[2,256,512]{2,1,0:T(8,128)(2,1)S(1)}, u32[]{:S(2)}, u32[]{:S(2)}) collective-permute-start(bf16[2,256,512]{2,1,0:T(8,128)(2,1)S(1)} %pad_maximum_fusion.6), channel_id=1, source_target_pairs={{0,4},{1,5},{2,6},{3,7},{4,0},{5,1},{6,2},{7,3},{8,12},{9,13},{10,... | collective-permute-start | bytes 1572872 | tf_op jit(solution)/shard_map/ppermute | solution.py:267
  (27 other events, 262.2 us)

commit v3 on v2

v3 whole, which is shorter than its diff:
```python
import jax
import jax.numpy as jnp
from jax import lax
from jax.experimental import pallas as pl
from jax.experimental.pallas import tpu as pltpu
from jax.sharding import PartitionSpec as P

HEADS = 8
HEAD = 128
EPS = 1e-05
VMEM = 56 * 2**20
F32 = jnp.float32
BF16 = jnp.bfloat16

NN = (((1,), (0,)), ((), ()))
NT = (((1,), (1,)), ((), ()))
TN = (((0,), (0,)), ((), ()))


def dot(a, b, dims=NN):
    return lax.dot_general(a, b, dims, preferred_element_type=F32)


def normalize(value):
    centred = value - jnp.mean(value, axis=-1, keepdims=True)
    spread = jnp.mean(centred * centred, axis=-1, keepdims=True)
    return centred * lax.rsqrt(spread + EPS)


def silu_grad(value):
    half = 0.5 * value
    th = jnp.tanh(half)
    return 0.5 * (1.0 + th) * (1.0 + half * (1.0 - th))


def history_start(bounds, row):
    return jnp.where(row >= bounds[1], bounds[1], jnp.where(row >= bounds[0], bounds[0], 0))


def proj_kernel(rows, starts, at_ref, *refs):
    count = len(starts)
    x_refs, w_ref = refs[:count], refs[count]
    normed_ref, pre_ref, act_ref, token_ref = refs[-4:]
    token_ref[...] = jnp.zeros_like(token_ref)
    for (other, start), x_ref in zip(starts, x_refs):
        size = x_ref.shape[0]
        core = 1 - at_ref[1] if other else at_ref[1]
        here = pl.ds(pl.multiple_of(core * rows + start, size), size)
        normed = normalize(x_ref[...].astype(F32)).astype(BF16)
        normed_ref[here, :] = normed
        pre = dot(normed, w_ref[...])
        pre_ref[here, :] = pre
        half = 0.5 * pre
        act_ref[here, :] = (half * (1.0 + jnp.tanh(half))).astype(BF16)


def fwd_kernel(rows, scale, order_ref, bounds_ref, act_ref, *refs):
    got_refs, (att_ref, stat_ref, cot_ref) = refs[:4], refs[4:]
    bounds = (bounds_ref[0], bounds_ref[1])
    wide = 2 * rows
    for s in range(2 * len(got_refs)):
        there = pl.ds(pl.multiple_of(order_ref[s] * rows, rows), rows)
        cot_ref[there, :] = got_refs[s // 2][s % 2, pl.ds(0, rows), :]

    def block(i, carry):
        row0 = pl.multiple_of(i * rows, rows)
        here = pl.ds(row0, rows)
        query = act_ref[here, pl.ds(0, HEAD)]
        end = row0 + rows
        row = row0 + lax.broadcasted_iota(jnp.int32, (rows, 1), 0)
        first = history_start(bounds, row)

        def inner(p, total):
            col0 = pl.multiple_of(jnp.maximum(end - (p + 1) * wide, 0), rows)
            there = pl.ds(col0, wide)
            keys = act_ref[there, pl.ds(HEAD, HEAD)]
            values = act_ref[there, pl.ds(2 * HEAD, HEAD)]
            t = dot(query, keys, NT) * (0.5 * scale)
            col = col0 + lax.broadcasted_iota(jnp.int32, (1, wide), 1)
            last = jnp.minimum(row, end - p * wide - 1)
            mask = (col <= last) & (col >= first)
            weights = jnp.where(mask, t * (1.0 + jnp.tanh(t)), 0.0).astype(BF16)
            return total + dot(weights, values)

        count = (end - history_start(bounds, row0) + wide - 1) // wide
        att = lax.fori_loop(0, count, inner, jnp.zeros((rows, HEAD), F32)) * (1.0 / 1024)
        att_t = att.T
        att_ref[:, here] = att_t
        cot_t = cot_ref[here, :].astype(F32).T
        mean = jnp.mean(att_t, axis=0, keepdims=True)
        centred = att_t - mean
        stat_ref[:, here] = jnp.concatenate(
            [
                mean,
                jnp.sum(centred * centred, axis=0, keepdims=True),
                jnp.sum(cot_t * centred, axis=0, keepdims=True),
                jnp.sum(cot_t, axis=0, keepdims=True),
            ],
            axis=0,
        )
        return carry

    lax.fori_loop(0, act_ref.shape[0] // rows, block, 0)


def bwd_kernel(rows, scale, inv_root, bounds_ref, order_ref, act_ref, att_ref, cot_ref, stat0_ref,
               stat1_ref, stat2_ref, stat3_ref, normed_any, pre_any, mine_ref, theirs_ref, gw_ref,
               normed_s, pre_s, sems, keys_t, n_s, dq_s, dk_s, dv_s, both_s, gw_s):
    bounds = (bounds_ref[0], bounds_ref[1])
    wide = 2 * rows
    width = HEADS * HEAD
    total = act_ref.shape[0]
    fetches = (
        pltpu.make_async_copy(normed_any, normed_s, sems.at[0]),
        pltpu.make_async_copy(pre_any, pre_s, sems.at[1]),
    )
    for fetch in fetches:
        fetch.start()
    dk_s[...] = jnp.zeros_like(dk_s)
    dv_s[...] = jnp.zeros_like(dv_s)
    keys_t[...] = act_ref[:, pl.ds(HEAD, HEAD)].T

    def block(i, carry):
        row0 = pl.multiple_of(i * rows, rows)
        here = pl.ds(row0, rows)
        end = row0 + rows
        stats = [ref[:, here] for ref in (stat0_ref, stat1_ref, stat2_ref, stat3_ref)]
        means, second, cross, sums = (
            jnp.concatenate([s[r + k : r + k + 1] for s in stats for r in (0, 4)], axis=0)
            for k in range(4)
        )
        mean = jnp.mean(means, axis=0, keepdims=True)
        shift = means - mean
        var = jnp.sum(second + HEAD * shift * shift, axis=0, keepdims=True) * (1.0 / width)
        factor = lax.rsqrt(var + EPS)
        mean_cot = jnp.sum(sums, axis=0, keepdims=True) * (1.0 / width)
        inner_mean = factor * jnp.sum(cross + shift * sums, axis=0, keepdims=True) * (1.0 / width)
        n_t = (att_ref[:, here] - mean) * factor
        cot_t = cot_ref[here, :].astype(F32).T
        ga_t = factor * (cot_t - mean_cot - n_t * inner_mean)
        n_s[here, :] = n_t.T.astype(BF16)
        grad_att = ga_t.T.astype(BF16)
        query = act_ref[here, pl.ds(0, HEAD)]
        row = row0 + lax.broadcasted_iota(jnp.int32, (1, rows), 1)
        first = history_start(bounds, row)

        def inner(p, total_q):
            col0 = pl.multiple_of(jnp.maximum(end - (p + 1) * wide, 0), rows)
            there = pl.ds(col0, wide)
            keys = act_ref[there, pl.ds(HEAD, HEAD)]
            values = act_ref[there, pl.ds(2 * HEAD, HEAD)]
            t = dot(keys, query, NT) * (0.5 * scale)
            prod = dot(values, grad_att, NT)
            col = col0 + lax.broadcasted_iota(jnp.int32, (wide, 1), 0)
            last = jnp.minimum(row, end - p * wide - 1)
            mask = (col <= last) & (col >= first)
            th = jnp.tanh(t)
            up = 1.0 + th
            weights = jnp.where(mask, t * up, 0.0).astype(BF16)
            grads = jnp.where(mask, prod * (up * (1.0 + t * (1.0 - th))), 0.0).astype(BF16)
            dv_s[there, :] += dot(weights, grad_att)
            dk_s[there, :] += dot(grads, query)
            return total_q + dot(keys_t[:, there], grads)

        count = (end - history_start(bounds, row0) + wide - 1) // wide
        dq_s[here, :] = lax.fori_loop(0, count, inner, jnp.zeros((HEAD, rows), F32)).T
        return carry

    lax.fori_loop(0, total // rows, block, 0)
    for fetch in fetches:
        fetch.wait()

    def late(i, carry):
        here = pl.ds(pl.multiple_of(i * wide, wide), wide)
        inv = 1.0 / 1024
        gpre = jnp.concatenate(
            [
                dq_s[here, :] * (0.5 * inv * scale),
                dk_s[here, :] * (0.5 * inv * scale),
                dv_s[here, :] * inv,
            ],
            axis=1,
        )
        gpre = (gpre * silu_grad(pre_s[here, :])).astype(BF16)
        both_s[:, pl.ds(0, HEAD)] = n_s[here, :]
        both_s[:, pl.ds(HEAD, 3 * HEAD)] = gpre
        mine_ref[i] = both_s[pl.ds(pl.multiple_of((order_ref[0] % 2) * rows, rows), rows), :]
        theirs_ref[i] = both_s[pl.ds(pl.multiple_of((1 - order_ref[0] % 2) * rows, rows), rows), :]
        term = dot(gpre, normed_s[here, :], TN)

        @pl.when(i == 0)
        def _():
            gw_s[...] = term

        @pl.when(i > 0)
        def _():
            gw_s[...] += term

        return carry

    lax.fori_loop(0, total // wide, late, 0)
    gw_ref[...] = (gw_s[...].T * inv_root).astype(BF16)


def out_kernel(rows, heads_ref, got0_ref, got1_ref, got2_ref, got3_ref, w_ref, x_ref, cot_ref,
               out_ref, gtok_ref, g_s, acc_s):
    step = pl.program_id(0)
    width = HEADS * HEAD
    part = w_ref.shape[0]

    @pl.when(step == 0)
    def _():
        for s, got_ref in enumerate((got0_ref, got1_ref, got2_ref, got3_ref)):
            for j in range(2):
                col = pl.multiple_of(heads_ref[2 * s + j] * HEAD, HEAD)
                out_ref[:, pl.ds(col, HEAD)] = (
                    x_ref[:, pl.ds(col, HEAD)].astype(F32) + got_ref[j, :, pl.ds(0, HEAD)].astype(F32)
                ).astype(BF16)
                for t in range(3):
                    g_s[:, pl.ds(t * width + col, HEAD)] = got_ref[j, :, pl.ds((t + 1) * HEAD, HEAD)]

    acc_s[step] = dot(g_s[...], w_ref[...], NT)

    @pl.when(step == pl.num_programs(0) - 1)
    def _():
        x = x_ref[...].astype(F32)
        centred = x - jnp.mean(x, axis=-1, keepdims=True)
        factor = lax.rsqrt(jnp.mean(centred * centred, axis=-1, keepdims=True) + EPS)
        normal = centred * factor
        grad = jnp.concatenate([acc_s[i] for i in range(width // part)], axis=1)
        back = factor * (
            grad
            - jnp.mean(grad, axis=-1, keepdims=True)
            - normal * jnp.mean(grad * normal, axis=-1, keepdims=True)
        )
        gtok_ref[...] = (cot_ref[...].astype(F32) + back).astype(BF16)


def join_kernel(piece, where_ref, *refs):
    same, other = refs[:4], refs[4:8]
    out_ref, buf, sem = refs[8:]
    step = pl.program_id(0)

    def fetch(q, wait):
        for side, group in enumerate((same, other)):
            rel = lax.rem(q - where_ref[side] + 4, 4)
            slot = lax.rem(q, 2)
            for a, ref in enumerate(group):

                @pl.when(rel == a)
                def _():
                    copy = pltpu.make_async_copy(ref, buf.at[slot, side], sem.at[slot, side])
                    copy.wait() if wait else copy.start()

    @pl.when(step == 0)
    def _():
        fetch(step, False)

    @pl.when(step + 1 < pl.num_programs(0))
    def _():
        fetch(step + 1, False)

    fetch(step, True)
    slot = lax.rem(step, 2)
    for side in range(2):
        for s in range(4):
            head = where_ref[2 + 4 * side + s]
            for t in range(3):
                col = pl.multiple_of((t * HEADS + head) * HEAD, HEAD)
                out_ref[:, pl.ds(col, HEAD)] = buf[slot, side, s, :, pl.ds(t * HEAD, HEAD)].astype(F32)


def params(n):
    return pltpu.CompilerParams(dimension_semantics=("arbitrary",) * n, vmem_limit_bytes=VMEM)


IN_VMEM = pl.BlockSpec(memory_space=pltpu.VMEM)
IN_SMEM = pl.BlockSpec(memory_space=pltpu.SMEM)
ANYWHERE = pl.BlockSpec(memory_space=pl.ANY)


def shape(dims, dtype):
    return jax.ShapeDtypeStruct(dims, dtype)


SIDE = 4


def ring(axis, step):
    pairs = []
    for place in range(2 * SIDE**3):
        core = place % 2
        at = [place // (2 * SIDE * SIDE), place // (2 * SIDE) % SIDE, place // 2 % SIDE]
        at[axis(core)] = (at[axis(core)] + step) % SIDE
        pairs.append((place, ((at[0] * SIDE + at[1]) * SIDE + at[2]) * 2 + core))
    return pairs


def along(axis):
    return lambda value, step: lax.ppermute(value, ("dp", "ctx"), ring(axis, step))


def along_z(value, step):
    return lax.ppermute(value, "ctx", [(c, (c + 2 * step) % 8) for c in range(8)])


def swap(value):
    return lax.ppermute(value, "ctx", [(c, c ^ 1) for c in range(8)])


def pick(value, index):
    return lax.dynamic_index_in_dim(value, index, 0, keepdims=False)


def exchange(mine, theirs, z):
    theirs = swap(theirs)
    send = lambda d: jnp.stack([pick(mine, (z + d) % SIDE), pick(theirs, (z + d) % SIDE)])
    from_far, from_before, from_after = (along_z(send(d), d) for d in (2, 1, -1))
    return send(0), from_before, from_after, from_far


def body(tokens, cotangent, proj_weight, segment):
    x_tok = tokens[0]
    grad_out = cotangent[0]
    seg_ids = segment[0]
    rows, width = x_tok.shape
    ctx_count = lax.axis_size("ctx")
    dp_count = lax.axis_size("dp")
    total = rows * ctx_count
    scale = 1.0 / HEAD**0.5
    inv_root = 1.0 / (dp_count * total) ** 0.5
    head = lax.axis_index("ctx")
    core, z = head % 2, head // 2
    x_at, y_at = lax.axis_index("dp") // SIDE, lax.axis_index("dp") % SIDE
    chips_at = [z, (z + 3) % SIDE, (z + 1) % SIDE, (z + 2) % SIDE]
    order = jnp.stack([2 * p + c for p in chips_at for c in (core, 1 - core)]).astype(jnp.int32)

    before = along_z(x_tok, 1)
    after = along_z(x_tok, -1)
    w_head = jnp.concatenate(
        [lax.dynamic_slice_in_dim(proj_weight, t * width + head * HEAD, HEAD, 1) for t in range(3)],
        axis=1,
    )

    def project(chip, starts, shards, earlier):
        return pl.pallas_call(
            lambda *refs: proj_kernel(rows, starts, *refs),
            grid_spec=pltpu.PrefetchScalarGridSpec(
                num_scalar_prefetch=1,
                grid=(1,),
                in_specs=[pl.BlockSpec(v.shape, lambda i, o: (0, 0)) for v in shards]
                + [pl.BlockSpec((width, 3 * HEAD), lambda i, o: (0, 0))]
                + [ANYWHERE] * len(earlier),
                out_specs=[
                    pl.BlockSpec((2 * rows, width), lambda i, o: (o[0], 0)),
                    pl.BlockSpec((2 * rows, 3 * HEAD), lambda i, o: (o[0], 0)),
                    pl.BlockSpec((2 * rows, 3 * HEAD), lambda i, o: (o[0], 0)),
                    pl.BlockSpec((8, HEAD), lambda i, o: (0, 0)),
                ],
            ),
            out_shape=[
                shape((total, width), BF16),
                shape((total, 3 * HEAD), F32),
                shape((total, 3 * HEAD), BF16),
                shape((8, HEAD), F32),
            ],
            input_output_aliases={2 + len(shards) + i: i for i in range(len(earlier))},
            compiler_params=params(1),
            cost_estimate=pl.CostEstimate(flops=1, bytes_accessed=1, transcendentals=0),
            name="project",
        )(jnp.stack([chip, core]).astype(jnp.int32), *shards, w_head, *earlier)

    after_token = lambda value, token: value + token[0, 0].astype(value.dtype)
    whole = ((0, 0), (1, 0))
    half = rows // 2
    *seen, token = project(z, whole, (x_tok, swap(x_tok)), ())
    far_low = along_z(after_token(before[:half], token), 1)
    far_high = along_z(after_token(after[half:], token), -1)

    counts = jnp.stack([jnp.sum(seg_ids < 1), jnp.sum(seg_ids < 2)]).astype(BF16)
    cot_chunks = jnp.concatenate(
        [
            grad_out.reshape(rows, HEADS, HEAD).transpose(1, 0, 2),
            jnp.broadcast_to(jnp.pad(counts, (0, HEAD - 2))[None, None], (HEADS, 16, HEAD)),
        ],
        axis=1,
    ).reshape(SIDE, 2, rows + 16, HEAD)
    cot_got = exchange(
        lax.dynamic_index_in_dim(cot_chunks, core, 1, keepdims=False),
        lax.dynamic_index_in_dim(cot_chunks, 1 - core, 1, keepdims=False),
        z,
    )
    bounds = sum(jnp.sum(v[:, rows, :2].astype(F32), axis=0) for v in cot_got).astype(jnp.int32)

    *seen, token = project(chips_at[1], whole, (before, swap(before)), seen)
    *seen, token = project(chips_at[2], whole, (after, swap(after)), seen)
    halves = ((0, 0), (0, half), (1, 0), (1, half))
    far = (far_low, far_high, swap(after_token(far_low, token)), swap(after_token(far_high, token)))
    normed, pre, act, token = project(chips_at[3], halves, far, seen)

    att_t, stat, cot_head = pl.pallas_call(
        lambda *refs: fwd_kernel(rows, scale, *refs),
        in_specs=[IN_SMEM, IN_SMEM] + [IN_VMEM] * 5,
        out_specs=[IN_VMEM] * 3,
        out_shape=[shape((HEAD, total), F32), shape((4, total), F32), shape((total, HEAD), BF16)],
        compiler_params=params(0),
        name="attend",
    )(order, bounds, act, *cot_got)

    pair = jnp.concatenate([stat, swap(stat)], axis=0)
    stats = (pair, along_z(pair, 2), along_z(pair, 1), along_z(pair, -1))

    mine, theirs, gw = pl.pallas_call(
        lambda *refs: bwd_kernel(rows, scale, inv_root, *refs),
        in_specs=[IN_SMEM, IN_SMEM] + [IN_VMEM] * 7 + [ANYWHERE] * 2,
        out_specs=[IN_VMEM] * 3,
        out_shape=[
            shape((SIDE, rows, 4 * HEAD), BF16),
            shape((SIDE, rows, 4 * HEAD), BF16),
            shape((width, 3 * HEAD), BF16),
        ],
        scratch_shapes=[
            pltpu.VMEM((total, width), BF16),
            pltpu.VMEM((total, 3 * HEAD), F32),
            pltpu.SemaphoreType.DMA((2,)),
            pltpu.VMEM((HEAD, total), BF16),
            pltpu.VMEM((total, HEAD), BF16),
            pltpu.VMEM((total, HEAD), F32),
            pltpu.VMEM((total, HEAD), F32),
            pltpu.VMEM((total, HEAD), F32),
            pltpu.VMEM((2 * rows, 4 * HEAD), BF16),
            pltpu.VMEM((3 * HEAD, width), F32),
        ],
        compiler_params=params(0),
        name="attend_back",
    )(bounds, order, act, att_t, cot_head, *stats, normed, pre)

    first_way = along(lambda c: c)
    other_way = along(lambda c: 1 - c)
    piece = width // SIDE
    my_piece = jnp.where(core == 0, x_at, y_at)
    cut = lambda d: lax.dynamic_slice_in_dim(gw, (my_piece + d) % SIDE * piece, piece, 0)
    up = lambda v: v.astype(F32)
    terms = [first_way(cut(d), d) for d in (2, 1, -1)]
    summed = ((up(cut(0)) + up(terms[0])) + (up(terms[1]) + up(terms[2]))).astype(BF16)
    terms = [other_way(summed, d) for d in (2, 1, -1)]
    summed = ((up(summed) + up(terms[0])) + (up(terms[1]) + up(terms[2]))).astype(BF16)
    got = exchange(mine, theirs, z)
    summed = summed + (0.0 * jnp.abs(got[3][0, 0, 0]).astype(F32)).astype(BF16)
    chips = jnp.stack([summed, along_z(summed, 1), along_z(summed, -1), along_z(summed, 2)])
    same = [chips, first_way(chips, -1), first_way(chips, 2), first_way(chips, 1)]
    other = [swap(v) for v in same]
    z_order = jnp.stack([z, (z + 3) % SIDE, (z + 1) % SIDE, (z + 2) % SIDE])
    where = jnp.concatenate(
        [
            jnp.stack([my_piece, jnp.where(core == 0, y_at, x_at)]),
            2 * z_order + core,
            2 * z_order + 1 - core,
        ]
    ).astype(jnp.int32)
    grad_weight = pl.pallas_call(
        lambda *refs: join_kernel(piece, *refs),
        grid_spec=pltpu.PrefetchScalarGridSpec(
            num_scalar_prefetch=1,
            grid=(SIDE,),
            in_specs=[pl.BlockSpec(memory_space=pl.ANY)] * 8,
            out_specs=pl.BlockSpec((piece, 3 * width), lambda i, w: (i, 0)),
            scratch_shapes=[
                pltpu.VMEM((2, 2, SIDE, piece, 3 * HEAD), BF16),
                pltpu.SemaphoreType.DMA((2, 2)),
            ],
        ),
        out_shape=jax.ShapeDtypeStruct((width, 3 * width), F32),
        compiler_params=params(1),
        name="join",
    )(where, *same, *other)

    part = 512
    output, grad_tok = pl.pallas_call(
        lambda *refs: out_kernel(rows, *refs),
        grid_spec=pltpu.PrefetchScalarGridSpec(
            num_scalar_prefetch=1,
            grid=(width // part,),
            in_specs=[pl.BlockSpec((2, rows, 4 * HEAD), lambda i, o: (0, 0, 0))] * 4
            + [
                pl.BlockSpec((part, 3 * width), lambda i, o: (i, 0)),
                pl.BlockSpec((rows, width), lambda i, o: (0, 0)),
                pl.BlockSpec((rows, width), lambda i, o: (0, 0)),
            ],
            out_specs=[
                pl.BlockSpec((rows, width), lambda i, o: (0, 0)),
                pl.BlockSpec((rows, width), lambda i, o: (0, 0)),
            ],
            scratch_shapes=[
                pltpu.VMEM((rows, 3 * width), BF16),
                pltpu.VMEM((width // part, rows, part), F32),
            ],
        ),
        out_shape=[jax.ShapeDtypeStruct((rows, width), BF16)] * 2,
        compiler_params=params(1),
        cost_estimate=pl.CostEstimate(flops=1, bytes_accessed=1, transcendentals=0),
        name="finish",
    )(order, *got, proj_weight, x_tok, grad_out)
    return (output[None], grad_tok[None], grad_weight)


def solution(mesh):
    in_specs = (P("dp", "ctx", None), P("dp", "ctx", None), P(), P("dp", "ctx"))
    out_specs = (P("dp", "ctx", None), P("dp", "ctx", None), P())
    return jax.shard_map(body, mesh=mesh, in_specs=in_specs, out_specs=out_specs, check_vma=False)
```

time: 214 us -> 190 us (0.89)
  waiting for transfers between devices: 59.3 us -> 39 us
  starting transfers between devices: 63.3 us -> 56.7 us
  other arithmetic: 11.8 us -> 15 us
    ppermute x19 -> x16, waiting for transfers between devices: 43.5 us -> 26.5 us  [along_z(): lax.ppermute(value, 'ctx', [(c, (c + 2 * step) % 8) for c in range(8)])]
    ppermute x13 -> x12, starting transfers between devices: 31 us -> 24.1 us  [swap(): return lax.ppermute(value, 'ctx', [(c, c ^ 1) for c in range(8)])]
    ppermute x9, waiting for transfers between devices: 13.6 us -> 10.3 us  [along(): lax.ppermute(value, ('dp', 'ctx'), ring(axis, step))]
    add x1 -> x5, other arithmetic: 0.01 us -> 2.79 us  [the longest x4 2.68 us: body(): after_token = lambda value, token: value + token[0, 0].astype(value.dtype)]
    another operation x12 -> x15, other arithmetic: 3.9 us -> 6.44 us  [the longest x4 2.51 us: project(): jnp.stack([chip, core]).astype(jnp.int32)]
    squeeze x2 -> x1, local copies, waits for them, and re-layouts: 2.29 us -> 0.03 us  [body(): lax.dynamic_index_in_dim(cot_chunks, 1 - core, 1, keepdims=False)]
    unnamed x45 -> x43, local copies, waits for them, and re-layouts: 7.56 us -> 5.7 us
    ppermute x19 -> x16, starting transfers between devices: 20.5 us -> 21 us  [along_z(): lax.ppermute(value, 'ctx', [(c, (c + 2 * step) % 8) for c in range(8)])]
  transfers between devices with their start and end apart: 41 -> 37, of which waited for: 15 -> 12; matrix products, arithmetic and copies ran while one was open for 7% -> 12% of each run, Pallas kernels for 4% -> 11%
where the time goes in v3:
time: 190 us; the launch traced here: 189 us
  Pallas kernels  62.5 us (33%)
  starting transfers between devices  56.7 us (30%)
  waiting for transfers between devices  39 us (21%)
  other arithmetic  15 us (8%)
  local copies, waits for them, and re-layouts  12.5 us (7%)
  between operations  3.16 us (2%)
    ppermute x16, waiting for transfers between devices, along_z(): lax.ppermute(value, 'ctx', [(c, (c + 2 * step) % 8) for c in range(8)])  26.5 us
    ppermute x12, starting transfers between devices, swap(): return lax.ppermute(value, 'ctx', [(c, c ^ 1) for c in range(8)])  24.1 us
    ppermute x16, starting transfers between devices, along_z(): lax.ppermute(value, 'ctx', [(c, (c + 2 * step) % 8) for c in range(8)])  21 us
    pallas_call x1, Pallas kernels, body(): pl.pallas_call(lambda *refs: bwd_kernel(rows, scale, inv_root, *refs), in...  18.3 us
    pallas_call x4, Pallas kernels, project(): pl.pallas_call(lambda *refs: proj_kernel(rows, starts, *refs), grid_spec=...  17.5 us
    ppermute x9, starting transfers between devices, along(): lax.ppermute(value, ('dp', 'ctx'), ring(axis, step))  11.6 us
    ppermute x9, waiting for transfers between devices, along(): lax.ppermute(value, ('dp', 'ctx'), ring(axis, step))  10.3 us
    pallas_call x1, Pallas kernels, body(): pl.pallas_call(lambda *refs: fwd_kernel(rows, scale, *refs), in_specs=[IN...  10.1 us
  transfers between devices with their start and end apart: 37, of which 12 were waited for; matrix products, arithmetic and copies ran while one was open for 12% of the time, Pallas kernels for 11%

profile of v3, /device:TPU:1, one launch (start us, length us, event | category | flops | bytes accessed | tf_op | source)
XLA Modules:
  0.0 188.8 jit_solution(8796536839784880533)
XLA Ops:
  0.6 1.5 collective-permute-start.5
  2.1 1.7 collective-permute-start.4
  3.9 2.1 %collective-permute-start.7 = (bf16[256,1024]{1,0:T(8,128)(2,1)}, bf16[256,1024]{1,0:T(8,128)(2,1)S(1)}, u32[]{:S(2)}, u32[]{:S(2)}) collective-permute-start(bf16[256,1024]{1,0:T(8,128)(2,1)} %bitcast.50), channel_id=1, source_target_pairs={{0,6},{1,7},{2,0},{3,1},{4,2},{5,3},{6,4},{7,5},{8,14},{9,15},{10,... | collective-permute-start | bytes 1572872 | tf_op jit(solution)/shard_map/ppermute | solution.py:304
  16.0 2.7 %collective-permute-start.2 = (bf16[2,272,128]{2,1,0:T(8,128)(2,1)S(1)}, bf16[2,272,128]{2,1,0:T(8,128)(2,1)S(1)}, u32[]{:S(2)}, u32[]{:S(2)}) collective-permute-start(bf16[2,272,128]{2,1,0:T(8,128)(2,1)S(1)} %pad_maximum_fusion.9), channel_id=1, source_target_pairs={{0,6},{1,7},{2,0},{3,1},{4,2},{5,3},{6,4},{7,5},{8,14},{9,15},{10,... | collective-permute-start | bytes 417800 | tf_op jit(solution)/shard_map/ppermute | solution.py:304
  19.5 2.9 %collective-permute-done.1.refs_4_ = bf16[2,272,128]{2,1,0:T(8,128)(2,1)S(1)} collective-permute-done((bf16[2,272,128]{2,1,0:T(8,128)(2,1)S(1)}, bf16[2,272,128]{2,1,0:T(8,128)(2,1)S(1)}, u32[]{:S(2)}, u32[]{:S(2)}) %collective-permute-start.1) | collective-permute-done | bytes 139296 | tf_op jit(solution)/shard_map/ppermute | solution.py:304
  23.5 4.3 %project.4 = (bf16[2048,1024]{1,0:T(8,128)(2,1)}, f32[2048,384]{1,0:T(8,128)}, bf16[2048,384]{1,0:T(8,128)(2,1)}, f32[8,128]{1,0:T(8,128)}) custom-call(s32[2]{0:T(128)} %pad_add_fusion.1.refs_0_, bf16[256,1024]{1,0:T(8,128)(2,1)} %bitcast.51, bf16[256,1024]{1,0:T(8,128)(2,1)} %copy-done.9, bf16[1024,384]{1,0:T(8,128)(2,1)} %pad_maximum_fusion.refs_3_.refs_5_), custom_call_target="tpu_custom_call" | custom-call | flops 1 | bytes 1 | tf_op jit(solution)/shard_map/project/pallas_call | solution.py:346
  34.1 4.3 %project.5 = (bf16[2048,1024]{1,0:T(8,128)(2,1)}, f32[2048,384]{1,0:T(8,128)}, bf16[2048,384]{1,0:T(8,128)(2,1)}, f32[8,128]{1,0:T(8,128)}) custom-call(s32[2]{0:T(128)} %pad_add_fusion.3.refs_0_, bf16[256,1024]{1,0:T(8,128)(2,1)} %copy-done.2, bf16[256,1024]{1,0:T(8,128)(2,1)} %copy-done.11, ...), custom_call_target="tpu_custom_call", output_to_operand_aliasing={{0}: (4, {}), {1}: (5, {}), {2}: (6, {})} | custom-call | flops 1 | bytes 1 | tf_op jit(solution)/shard_map/project/pallas_call | solution.py:346
  39.2 4.3 %project.6 = (bf16[2048,1024]{1,0:T(8,128)(2,1)}, f32[2048,384]{1,0:T(8,128)}, bf16[2048,384]{1,0:T(8,128)(2,1)}, f32[8,128]{1,0:T(8,128)}) custom-call(s32[2]{0:T(128)} %pad_add_fusion.2.refs_0_, bf16[256,1024]{1,0:T(8,128)(2,1)} %copy-done.1, bf16[256,1024]{1,0:T(8,128)(2,1)} %copy-done.10, ...), custom_call_target="tpu_custom_call", output_to_operand_aliasing={{0}: (4, {}), {1}: (5, {}), {2}: (6, {})} | custom-call | flops 1 | bytes 1 | tf_op jit(solution)/shard_map/project/pallas_call | solution.py:346
  49.6 4.5 %project.7 = (bf16[2048,1024]{1,0:T(8,128)(2,1)}, f32[2048,384]{1,0:T(8,128)}, bf16[2048,384]{1,0:T(8,128)(2,1)}, f32[8,128]{1,0:T(8,128)}) custom-call(s32[2]{0:T(128)} %pad_add_fusion.refs_0_, bf16[128,1024]{1,0:T(8,128)(2,1)} %copy-done.4, bf16[128,1024]{1,0:T(8,128)(2,1)} %copy-done.3, ...), custom_call_target="tpu_custom_call", output_to_operand_aliasing={{0}: (6, {}), {1}: (7, {}), {2}: (8, {})} | custom-call | flops 1 | bytes 1 | tf_op jit(solution)/shard_map/project/pallas_call | solution.py:346
  54.1 10.1 %attend.1 = (f32[128,2048]{1,0:T(8,128)}, f32[4,2048]{1,0:T(4,128)}, bf16[2048,128]{1,0:T(8,128)(2,1)}) custom-call(s32[8]{0:T(128)} %stack.145.refs_0_.refs_1_, s32[2]{0:T(128)} %add_convert_fusion.2.refs_1_.refs_0_, bf16[2048,384]{1,0:T(8,128)(2,1)} %get-tuple-element.36.refs_2_, bf16[2,272,128]{2,1,0:T(8,128)(2,1)} %pad_maximum_fusion.7.refs_3_, ...), custom_call_target="tpu_custom_call" | custom-call | tf_op jit(solution)/shard_map/attend/pallas_call | solution.py:401
  66.4 2.8 %collective-permute-start.14 = (f32[8,2048]{1,0:T(8,128)S(1)}, f32[8,2048]{1,0:T(8,128)S(1)}, u32[]{:S(2)}, u32[]{:S(2)}) collective-permute-start(f32[8,2048]{1,0:T(8,128)S(1)} %pad_maximum_fusion.11.refs_5_), channel_id=1, source_target_pairs={{0,4},{1,5},{2,6},{3,7},{4,0},{5,1},{6,2},{7,3},{8,12},{9,13},{10,... | collective-permute-start | bytes 196616 | tf_op jit(solution)/shard_map/ppermute | solution.py:304
  69.2 2.7 %collective-permute-start.16 = (f32[8,2048]{1,0:T(8,128)S(1)}, f32[8,2048]{1,0:T(8,128)S(1)}, u32[]{:S(2)}, u32[]{:S(2)}) collective-permute-start(f32[8,2048]{1,0:T(8,128)S(1)} %pad_maximum_fusion.11.refs_5_), channel_id=1, source_target_pairs={{0,6},{1,7},{2,0},{3,1},{4,2},{5,3},{6,4},{7,5},{8,14},{9,15},{10,... | collective-permute-start | bytes 196616 | tf_op jit(solution)/shard_map/ppermute | solution.py:304
  71.8 1.6 collective-permute-done.15.refs_7_
  74.1 18.3 %attend_back.1 = (bf16[4,256,512]{2,1,0:T(8,128)(2,1)}, bf16[4,256,512]{2,1,0:T(8,128)(2,1)}, bf16[1024,384]{1,0:T(8,128)(2,1)}) custom-call(s32[2]{0:T(128)} %add_convert_fusion.2.refs_1_.refs_0_, s32[8]{0:T(128)} %stack.145.refs_0_.refs_1_, bf16[2048,384]{1,0:T(8,128)(2,1)} %get-tuple-element.36.refs_2_, f32[128,2048]{1,0:T(8,128)} %get-tuple-element.37.refs_3_, ...), custom_call_target="tpu_custom_call" | custom-call | tf_op jit(solution)/shard_map/attend_back/pallas_call | solution.py:413
  92.5 1.7 collective-permute-start.17
  94.1 1.9 constant_dynamic-slice_fusion.2
  97.1 2.3 %collective-permute-start.23 = (bf16[256,384]{1,0:T(8,128)(2,1)S(1)}, bf16[256,384]{1,0:T(8,128)(2,1)}, u32[]{:S(2)}, u32[]{:S(2)}) collective-permute-start(bf16[256,384]{1,0:T(8,128)(2,1)S(1)} %get-tuple-element.63), channel_id=1, source_target_pairs={{0,96},{1,25},{2,98},{3,27},{4,100},{5,29},{6,102},{7,31},{8,104},... | collective-permute-start | bytes 589832 | tf_op jit(solution)/shard_map/ppermute | solution.py:300
  102.6 2.1 %collective-permute-done.22 = bf16[256,384]{1,0:T(8,128)(2,1)S(1)} collective-permute-done((bf16[256,384]{1,0:T(8,128)(2,1)S(1)}, bf16[256,384]{1,0:T(8,128)(2,1)S(1)}, u32[]{:S(2)}, u32[]{:S(2)}) %collective-permute-start.22) | collective-permute-done | bytes 196640 | tf_op jit(solution)/shard_map/ppermute | solution.py:300
  105.8 2.1 %collective-permute-start.24 = (bf16[256,384]{1,0:T(8,128)(2,1)S(1)}, bf16[256,384]{1,0:T(8,128)(2,1)S(1)}, u32[]{:S(2)}, u32[]{:S(2)}) collective-permute-start(bf16[256,384]{1,0:T(8,128)(2,1)S(1)} %add_convert_fusion.1), channel_id=1, source_target_pairs={{0,16},{1,65},{2,18},{3,67},{4,20},{5,69},{6,22},{7,71},{8,24},{9,... | collective-permute-start | bytes 589832 | tf_op jit(solution)/shard_map/ppermute | solution.py:300
  107.8 1.5 collective-permute-start.25
  110.5 3.5 %collective-permute-done.20.refs_4_ = bf16[2,256,512]{2,1,0:T(8,128)(2,1)S(1)} collective-permute-done((bf16[2,256,512]{2,1,0:T(8,128)(2,1)S(1)}, bf16[2,256,512]{2,1,0:T(8,128)(2,1)S(1)}, u32[]{:S(2)}, u32[]{:S(2)}) %collective-permute-start.20) | collective-permute-done | bytes 524320 | tf_op jit(solution)/shard_map/ppermute | solution.py:304
  116.2 2.2 %collective-permute-start.28 = (bf16[256,384]{1,0:T(8,128)(2,1)S(1)}, bf16[256,384]{1,0:T(8,128)(2,1)S(1)}, u32[]{:S(2)}, u32[]{:S(2)}) collective-permute-start(bf16[256,384]{1,0:T(8,128)(2,1)S(1)} %fusion), channel_id=1, source_target_pairs={{0,6},{1,7},{2,0},{3,1},{4,2},{5,3},{6,4},{7,5},{8,14},{9,15},{10,... | collective-permute-start | bytes 589832 | tf_op jit(solution)/shard_map/ppermute | solution.py:304
  119.5 1.9 collective-permute-done.27
  121.8 3.8 %collective-permute-done.29 = bf16[256,384]{1,0:T(8,128)(2,1)S(1)} collective-permute-done((bf16[256,384]{1,0:T(8,128)(2,1)S(1)}, bf16[256,384]{1,0:T(8,128)(2,1)S(1)}, u32[]{:S(2)}, u32[]{:S(2)}) %collective-permute-start.29) | collective-permute-done | bytes 196640 | tf_op jit(solution)/shard_map/ppermute | solution.py:304
  125.8 2.8 %collective-permute-start.30 = (bf16[4,256,384]{2,1,0:T(8,128)(2,1)S(1)}, bf16[4,256,384]{2,1,0:T(8,128)(2,1)S(1)}, u32[]{:S(2)}, u32[]{:S(2)}) collective-permute-start(bf16[4,256,384]{2,1,0:T(8,128)(2,1)S(1)} %pad_maximum_fusion.1.refs_1_), channel_id=1, source_target_pairs={{0,96},{1,25},{2,98},{3,27},{4,100},{5,29},{6,102},{7,31},{8,104},... | collective-permute-start | bytes 2359304 | tf_op jit(solution)/shard_map/ppermute | solution.py:300
  130.8 7.5 %collective-permute-start.33 = (bf16[4,256,384]{2,1,0:T(8,128)(2,1)S(1)}, bf16[4,256,384]{2,1,0:T(8,128)(2,1)}, u32[]{:S(2)}, u32[]{:S(2)}) collective-permute-start(bf16[4,256,384]{2,1,0:T(8,128)(2,1)S(1)} %pad_maximum_fusion.1.refs_1_), channel_id=1, source_target_pairs={{0,1},{1,0},{2,3},{3,2},{4,5},{5,4},{6,7},{7,6},{8,9},{9,8},{10,11... | collective-permute-start | bytes 2359304 | tf_op jit(solution)/shard_map/ppermute | solution.py:308
  138.2 7.7 %collective-permute-done.30.refs_2_ = bf16[4,256,384]{2,1,0:T(8,128)(2,1)S(1)} collective-permute-done((bf16[4,256,384]{2,1,0:T(8,128)(2,1)S(1)}, bf16[4,256,384]{2,1,0:T(8,128)(2,1)S(1)}, u32[]{:S(2)}, u32[]{:S(2)}) %collective-permute-start.30) | collective-permute-done | bytes 786464 | tf_op jit(solution)/shard_map/ppermute | solution.py:300
  145.9 6.3 %collective-permute-start.34 = (bf16[4,256,384]{2,1,0:T(8,128)(2,1)S(1)}, bf16[4,256,384]{2,1,0:T(8,128)(2,1)}, u32[]{:S(2)}, u32[]{:S(2)}) collective-permute-start(bf16[4,256,384]{2,1,0:T(8,128)(2,1)S(1)} %collective-permute-done.30.refs_2_), channel_id=1, source_target_pairs={{0,1},{1,0},{2,3},{3,2},{4,5},{5,4},{6,7},{7,6},{8,9},{9,8},{10,11... | collective-permute-start | bytes 2359304 | tf_op jit(solution)/shard_map/ppermute | solution.py:308
  152.3 4.0 %collective-permute-start.36 = (bf16[4,256,384]{2,1,0:T(8,128)(2,1)}, bf16[4,256,384]{2,1,0:T(8,128)(2,1)}, u32[]{:S(2)}, u32[]{:S(2)}) collective-permute-start(bf16[4,256,384]{2,1,0:T(8,128)(2,1)} %collective-permute-done.32.refs_4_), channel_id=1, source_target_pairs={{0,1},{1,0},{2,3},{3,2},{4,5},{5,4},{6,7},{7,6},{8,9},{9,8},{10,11... | collective-permute-start | bytes 2359304 | tf_op jit(solution)/shard_map/ppermute | solution.py:308
  158.8 12.4 %collective-permute-done.18.refs_2_ = bf16[2,256,512]{2,1,0:T(8,128)(2,1)S(1)} collective-permute-done((bf16[2,256,512]{2,1,0:T(8,128)(2,1)S(1)}, bf16[2,256,512]{2,1,0:T(8,128)(2,1)S(1)}, u32[]{:S(2)}, u32[]{:S(2)}) %collective-permute-start.18) | collective-permute-done | bytes 524320 | tf_op jit(solution)/shard_map/ppermute | solution.py:304
  172.0 7.7 %finish.1 = (bf16[256,1024]{1,0:T(8,128)(2,1)}, bf16[256,1024]{1,0:T(8,128)(2,1)}) custom-call(s32[8]{0:T(128)} %stack.145.refs_0_.refs_1_, bf16[2,256,512]{2,1,0:T(8,128)(2,1)} %pad_maximum_fusion.3.refs_1_, bf16[2,256,512]{2,1,0:T(8,128)(2,1)} %copy-done.8, bf16[2,256,512]{2,1,0:T(8,128)(2,1)} %copy-done.7, bf16[2,256,512]{2,1,0:T(8,128)(2,1)} %copy-done.6, ...), custom_call_target="tpu_custom_call" | custom-call | flops 1 | bytes 1 | tf_op jit(solution)/shard_map/finish/pallas_call | solution.py:479
  179.7 8.9 %join.1 = f32[1024,3072]{1,0:T(8,128)} custom-call(s32[10]{0:T(128)} %pad_add_fusion.4.refs_0_, bf16[4,256,384]{2,1,0:T(8,128)(2,1)} %copy-done, bf16[4,256,384]{2,1,0:T(8,128)(2,1)} %copy-done.5, bf16[4,256,384]{2,1,0:T(8,128)(2,1)} %collective-permute-done.31.refs_3_, bf16[4,256,384]{2,1,0:T(8,128)(2,1)} %collective-permute-done.32.refs_4_, ...), custom_call_target="tpu_custom_call" | custom-call | tf_op jit(solution)/shard_map/join/pallas_call | solution.py:461
  (140 shorter events, 41.8 us)
Async XLA Ops:
  0.6 22.0 %collective-permute-start.5 = (bf16[256,1024]{1,0:T(8,128)(2,1)}, bf16[256,1024]{1,0:T(8,128)(2,1)S(1)}, u32[]{:S(2)}, u32[]{:S(2)}) collective-permute-start(bf16[256,1024]{1,0:T(8,128)(2,1)} %bitcast.48), channel_id=1, source_target_pairs={{0,1},{1,0},{2,3},{3,2},{4,5},{5,4},{6,7},{7,6},{8,9},{9,8},{10,11... | collective-permute-start | bytes 1572872 | tf_op jit(solution)/shard_map/ppermute | solution.py:308
  2.1 26.9 %collective-permute-start.4 = (bf16[256,1024]{1,0:T(8,128)(2,1)}, bf16[256,1024]{1,0:T(8,128)(2,1)S(1)}, u32[]{:S(2)}, u32[]{:S(2)}) collective-permute-start(bf16[256,1024]{1,0:T(8,128)(2,1)} %bitcast.49), channel_id=1, source_target_pairs={{0,2},{1,3},{2,4},{3,5},{4,6},{5,7},{6,0},{7,1},{8,10},{9,11},{10,... | collective-permute-start | bytes 1572872 | tf_op jit(solution)/shard_map/ppermute | solution.py:304
  3.9 26.4 %collective-permute-start.7 = (bf16[256,1024]{1,0:T(8,128)(2,1)}, bf16[256,1024]{1,0:T(8,128)(2,1)S(1)}, u32[]{:S(2)}, u32[]{:S(2)}) collective-permute-start(bf16[256,1024]{1,0:T(8,128)(2,1)} %bitcast.50), channel_id=1, source_target_pairs={{0,6},{1,7},{2,0},{3,1},{4,2},{5,3},{6,4},{7,5},{8,14},{9,15},{10,... | collective-permute-start | bytes 1572872 | tf_op jit(solution)/shard_map/ppermute | solution.py:304
  10.0 5.9 %collective-permute-start = (bf16[4,272,128]{2,1,0:T(8,128)(2,1)S(1)}, bf16[4,272,128]{2,1,0:T(8,128)(2,1)S(1)}, u32[]{:S(2)}, u32[]{:S(2)}) collective-permute-start(bf16[4,272,128]{2,1,0:T(8,128)(2,1)S(1)} %dynamic-slice_bitcast_fusion), channel_id=1, source_target_pairs={{0,1},{1,0},{2,3},{3,2},{4,5},{5,4},{6,7},{7,6},{8,9},{9,8},{10,11... | collective-permute-start | bytes 835592 | tf_op jit(solution)/shard_map/ppermute | solution.py:308
  15.9 6.4 %collective-permute-start.1 = (bf16[2,272,128]{2,1,0:T(8,128)(2,1)S(1)}, bf16[2,272,128]{2,1,0:T(8,128)(2,1)S(1)}, u32[]{:S(2)}, u32[]{:S(2)}) collective-permute-start(bf16[2,272,128]{2,1,0:T(8,128)(2,1)S(1)} %pad_maximum_fusion.8), channel_id=1, source_target_pairs={{0,2},{1,3},{2,4},{3,5},{4,6},{5,7},{6,0},{7,1},{8,10},{9,11},{10,... | collective-permute-start | bytes 417800 | tf_op jit(solution)/shard_map/ppermute | solution.py:304
  16.0 16.6 %collective-permute-start.2 = (bf16[2,272,128]{2,1,0:T(8,128)(2,1)S(1)}, bf16[2,272,128]{2,1,0:T(8,128)(2,1)S(1)}, u32[]{:S(2)}, u32[]{:S(2)}) collective-permute-start(bf16[2,272,128]{2,1,0:T(8,128)(2,1)S(1)} %pad_maximum_fusion.9), channel_id=1, source_target_pairs={{0,6},{1,7},{2,0},{3,1},{4,2},{5,3},{6,4},{7,5},{8,14},{9,15},{10,... | collective-permute-start | bytes 417800 | tf_op jit(solution)/shard_map/ppermute | solution.py:304
  22.4 25.1 %collective-permute-start.3 = (bf16[2,272,128]{2,1,0:T(8,128)(2,1)S(1)}, bf16[2,272,128]{2,1,0:T(8,128)(2,1)S(1)}, u32[]{:S(2)}, u32[]{:S(2)}) collective-permute-start(bf16[2,272,128]{2,1,0:T(8,128)(2,1)S(1)} %pad_maximum_fusion.10), channel_id=1, source_target_pairs={{0,4},{1,5},{2,6},{3,7},{4,0},{5,1},{6,2},{7,3},{8,12},{9,13},{10,... | collective-permute-start | bytes 417800 | tf_op jit(solution)/shard_map/ppermute | solution.py:304
  30.2 8.2 %collective-permute-start.9 = (bf16[256,1024]{1,0:T(8,128)(2,1)S(1)}, bf16[256,1024]{1,0:T(8,128)(2,1)S(1)}, u32[]{:S(2)}, u32[]{:S(2)}) collective-permute-start(bf16[256,1024]{1,0:T(8,128)(2,1)S(1)} %collective-permute-done.7.refs_1_), channel_id=1, source_target_pairs={{0,1},{1,0},{2,3},{3,2},{4,5},{5,4},{6,7},{7,6},{8,9},{9,8},{10,11... | collective-permute-start | bytes 1572872 | tf_op jit(solution)/shard_map/ppermute | solution.py:308
  31.0 13.8 %collective-permute-start.8 = (bf16[128,1024]{1,0:T(8,128)(2,1)S(1)}, bf16[128,1024]{1,0:T(8,128)(2,1)S(1)}, u32[]{:S(2)}, u32[]{:S(2)}) collective-permute-start(bf16[128,1024]{1,0:T(8,128)(2,1)S(1)} %slice_add_fusion), channel_id=1, source_target_pairs={{0,6},{1,7},{2,0},{3,1},{4,2},{5,3},{6,4},{7,5},{8,14},{9,15},{10,... | collective-permute-start | bytes 786440 | tf_op jit(solution)/shard_map/ppermute | solution.py:304
  32.6 14.0 %collective-permute-start.6 = (bf16[128,1024]{1,0:T(8,128)(2,1)S(1)}, bf16[128,1024]{1,0:T(8,128)(2,1)S(1)}, u32[]{:S(2)}, u32[]{:S(2)}) collective-permute-start(bf16[128,1024]{1,0:T(8,128)(2,1)S(1)} %slice_add_fusion.1), channel_id=1, source_target_pairs={{0,2},{1,3},{2,4},{3,5},{4,6},{5,7},{6,0},{7,1},{8,10},{9,11},{10,... | collective-permute-start | bytes 786440 | tf_op jit(solution)/shard_map/ppermute | solution.py:304
  66.4 5.4 %collective-permute-start.14 = (f32[8,2048]{1,0:T(8,128)S(1)}, f32[8,2048]{1,0:T(8,128)S(1)}, u32[]{:S(2)}, u32[]{:S(2)}) collective-permute-start(f32[8,2048]{1,0:T(8,128)S(1)} %pad_maximum_fusion.11.refs_5_), channel_id=1, source_target_pairs={{0,4},{1,5},{2,6},{3,7},{4,0},{5,1},{6,2},{7,3},{8,12},{9,13},{10,... | collective-permute-start | bytes 196616 | tf_op jit(solution)/shard_map/ppermute | solution.py:304
  69.2 4.3 %collective-permute-start.15 = (f32[8,2048]{1,0:T(8,128)S(1)}, f32[8,2048]{1,0:T(8,128)S(1)}, u32[]{:S(2)}, u32[]{:S(2)}) collective-permute-start(f32[8,2048]{1,0:T(8,128)S(1)} %pad_maximum_fusion.11.refs_5_), channel_id=1, source_target_pairs={{0,2},{1,3},{2,4},{3,5},{4,6},{5,7},{6,0},{7,1},{8,10},{9,11},{10,... | collective-permute-start | bytes 196616 | tf_op jit(solution)/shard_map/ppermute | solution.py:304
  92.5 8.2 %collective-permute-start.17 = (bf16[4,256,512]{2,1,0:T(8,128)(2,1)}, bf16[4,256,512]{2,1,0:T(8,128)(2,1)S(1)}, u32[]{:S(2)}, u32[]{:S(2)}) collective-permute-start(bf16[4,256,512]{2,1,0:T(8,128)(2,1)} %get-tuple-element.43), channel_id=1, source_target_pairs={{0,1},{1,0},{2,3},{3,2},{4,5},{5,4},{6,7},{7,6},{8,9},{9,8},{10,11... | collective-permute-start | bytes 3145736 | tf_op jit(solution)/shard_map/ppermute | solution.py:308
  96.0 6.6 %collective-permute-start.21 = (bf16[256,384]{1,0:T(8,128)(2,1)}, bf16[256,384]{1,0:T(8,128)(2,1)S(1)}, u32[]{:S(2)}, u32[]{:S(2)}) collective-permute-start(bf16[256,384]{1,0:T(8,128)(2,1)} %get-tuple-element.62), channel_id=1, source_target_pairs={{0,64},{1,17},{2,66},{3,19},{4,68},{5,21},{6,70},{7,23},{8,72},{9,... | collective-permute-start | bytes 589832 | tf_op jit(solution)/shard_map/ppermute | solution.py:300
  96.7 7.9 %collective-permute-start.22 = (bf16[256,384]{1,0:T(8,128)(2,1)S(1)}, bf16[256,384]{1,0:T(8,128)(2,1)S(1)}, u32[]{:S(2)}, u32[]{:S(2)}) collective-permute-start(bf16[256,384]{1,0:T(8,128)(2,1)S(1)} %get-tuple-element.64), channel_id=1, source_target_pairs={{0,32},{1,9},{2,34},{3,11},{4,36},{5,13},{6,38},{7,15},{8,40},{9,1... | collective-permute-start | bytes 589832 | tf_op jit(solution)/shard_map/ppermute | solution.py:300
  97.1 7.5 %collective-permute-start.23 = (bf16[256,384]{1,0:T(8,128)(2,1)S(1)}, bf16[256,384]{1,0:T(8,128)(2,1)}, u32[]{:S(2)}, u32[]{:S(2)}) collective-permute-start(bf16[256,384]{1,0:T(8,128)(2,1)S(1)} %get-tuple-element.63), channel_id=1, source_target_pairs={{0,96},{1,25},{2,98},{3,27},{4,100},{5,29},{6,102},{7,31},{8,104},... | collective-permute-start | bytes 589832 | tf_op jit(solution)/shard_map/ppermute | solution.py:300
  100.9 13.1 %collective-permute-start.20 = (bf16[2,256,512]{2,1,0:T(8,128)(2,1)S(1)}, bf16[2,256,512]{2,1,0:T(8,128)(2,1)S(1)}, u32[]{:S(2)}, u32[]{:S(2)}) collective-permute-start(bf16[2,256,512]{2,1,0:T(8,128)(2,1)S(1)} %pad_maximum_fusion.6), channel_id=1, source_target_pairs={{0,4},{1,5},{2,6},{3,7},{4,0},{5,1},{6,2},{7,3},{8,12},{9,13},{10,... | collective-permute-start | bytes 1572872 | tf_op jit(solution)/shard_map/ppermute | solution.py:304
  105.8 9.4 %collective-permute-start.24 = (bf16[256,384]{1,0:T(8,128)(2,1)S(1)}, bf16[256,384]{1,0:T(8,128)(2,1)S(1)}, u32[]{:S(2)}, u32[]{:S(2)}) collective-permute-start(bf16[256,384]{1,0:T(8,128)(2,1)S(1)} %add_convert_fusion.1), channel_id=1, source_target_pairs={{0,16},{1,65},{2,18},{3,67},{4,20},{5,69},{6,22},{7,71},{8,24},{9,... | collective-permute-start | bytes 589832 | tf_op jit(solution)/shard_map/ppermute | solution.py:300
  107.8 7.4 %collective-permute-start.25 = (bf16[256,384]{1,0:T(8,128)(2,1)S(1)}, bf16[256,384]{1,0:T(8,128)(2,1)S(1)}, u32[]{:S(2)}, u32[]{:S(2)}) collective-permute-start(bf16[256,384]{1,0:T(8,128)(2,1)S(1)} %add_convert_fusion.1), channel_id=1, source_target_pairs={{0,8},{1,33},{2,10},{3,35},{4,12},{5,37},{6,14},{7,39},{8,16},{9,4... | collective-permute-start | bytes 589832 | tf_op jit(solution)/shard_map/ppermute | solution.py:300
  109.4 5.9 %collective-permute-start.26 = (bf16[256,384]{1,0:T(8,128)(2,1)S(1)}, bf16[256,384]{1,0:T(8,128)(2,1)S(1)}, u32[]{:S(2)}, u32[]{:S(2)}) collective-permute-start(bf16[256,384]{1,0:T(8,128)(2,1)S(1)} %add_convert_fusion.1), channel_id=1, source_target_pairs={{0,24},{1,97},{2,26},{3,99},{4,28},{5,101},{6,30},{7,103},{8,0},{9... | collective-permute-start | bytes 589832 | tf_op jit(solution)/shard_map/ppermute | solution.py:300
  115.4 6.0 %collective-permute-start.27 = (bf16[256,384]{1,0:T(8,128)(2,1)S(1)}, bf16[256,384]{1,0:T(8,128)(2,1)S(1)}, u32[]{:S(2)}, u32[]{:S(2)}) collective-permute-start(bf16[256,384]{1,0:T(8,128)(2,1)S(1)} %fusion), channel_id=1, source_target_pairs={{0,2},{1,3},{2,4},{3,5},{4,6},{5,7},{6,0},{7,1},{8,10},{9,11},{10,... | collective-permute-start | bytes 589832 | tf_op jit(solution)/shard_map/ppermute | solution.py:304
  116.2 5.6 %collective-permute-start.28 = (bf16[256,384]{1,0:T(8,128)(2,1)S(1)}, bf16[256,384]{1,0:T(8,128)(2,1)S(1)}, u32[]{:S(2)}, u32[]{:S(2)}) collective-permute-start(bf16[256,384]{1,0:T(8,128)(2,1)S(1)} %fusion), channel_id=1, source_target_pairs={{0,6},{1,7},{2,0},{3,1},{4,2},{5,3},{6,4},{7,5},{8,14},{9,15},{10,... | collective-permute-start | bytes 589832 | tf_op jit(solution)/shard_map/ppermute | solution.py:304
  118.4 7.2 %collective-permute-start.29 = (bf16[256,384]{1,0:T(8,128)(2,1)S(1)}, bf16[256,384]{1,0:T(8,128)(2,1)S(1)}, u32[]{:S(2)}, u32[]{:S(2)}) collective-permute-start(bf16[256,384]{1,0:T(8,128)(2,1)S(1)} %fusion), channel_id=1, source_target_pairs={{0,4},{1,5},{2,6},{3,7},{4,0},{5,1},{6,2},{7,3},{8,12},{9,13},{10,... | collective-permute-start | bytes 589832 | tf_op jit(solution)/shard_map/ppermute | solution.py:304
  125.8 20.1 %collective-permute-start.30 = (bf16[4,256,384]{2,1,0:T(8,128)(2,1)S(1)}, bf16[4,256,384]{2,1,0:T(8,128)(2,1)S(1)}, u32[]{:S(2)}, u32[]{:S(2)}) collective-permute-start(bf16[4,256,384]{2,1,0:T(8,128)(2,1)S(1)} %pad_maximum_fusion.1.refs_1_), channel_id=1, source_target_pairs={{0,96},{1,25},{2,98},{3,27},{4,100},{5,29},{6,102},{7,31},{8,104},... | collective-permute-start | bytes 2359304 | tf_op jit(solution)/shard_map/ppermute | solution.py:300
  128.6 23.6 %collective-permute-start.31 = (bf16[4,256,384]{2,1,0:T(8,128)(2,1)S(1)}, bf16[4,256,384]{2,1,0:T(8,128)(2,1)}, u32[]{:S(2)}, u32[]{:S(2)}) collective-permute-start(bf16[4,256,384]{2,1,0:T(8,128)(2,1)S(1)} %pad_maximum_fusion.1.refs_1_), channel_id=1, source_target_pairs={{0,64},{1,17},{2,66},{3,19},{4,68},{5,21},{6,70},{7,23},{8,72},{9,... | collective-permute-start | bytes 2359304 | tf_op jit(solution)/shard_map/ppermute | solution.py:300
  128.6 23.7 %collective-permute-start.32 = (bf16[4,256,384]{2,1,0:T(8,128)(2,1)S(1)}, bf16[4,256,384]{2,1,0:T(8,128)(2,1)}, u32[]{:S(2)}, u32[]{:S(2)}) collective-permute-start(bf16[4,256,384]{2,1,0:T(8,128)(2,1)S(1)} %pad_maximum_fusion.1.refs_1_), channel_id=1, source_target_pairs={{0,32},{1,9},{2,34},{3,11},{4,36},{5,13},{6,38},{7,15},{8,40},{9,1... | collective-permute-start | bytes 2359304 | tf_op jit(solution)/shard_map/ppermute | solution.py:300
  130.1 26.3 %collective-permute-start.19 = (bf16[2,256,512]{2,1,0:T(8,128)(2,1)}, bf16[2,256,512]{2,1,0:T(8,128)(2,1)S(1)}, u32[]{:S(2)}, u32[]{:S(2)}) collective-permute-start(bf16[2,256,512]{2,1,0:T(8,128)(2,1)} %pad_maximum_fusion.5), channel_id=1, source_target_pairs={{0,6},{1,7},{2,0},{3,1},{4,2},{5,3},{6,4},{7,5},{8,14},{9,15},{10,... | collective-permute-start | bytes 1572872 | tf_op jit(solution)/shard_map/ppermute | solution.py:304
  130.8 49.0 %collective-permute-start.33 = (bf16[4,256,384]{2,1,0:T(8,128)(2,1)S(1)}, bf16[4,256,384]{2,1,0:T(8,128)(2,1)}, u32[]{:S(2)}, u32[]{:S(2)}) collective-permute-start(bf16[4,256,384]{2,1,0:T(8,128)(2,1)S(1)} %pad_maximum_fusion.1.refs_1_), channel_id=1, source_target_pairs={{0,1},{1,0},{2,3},{3,2},{4,5},{5,4},{6,7},{7,6},{8,9},{9,8},{10,11... | collective-permute-start | bytes 2359304 | tf_op jit(solution)/shard_map/ppermute | solution.py:308
  145.9 33.8 %collective-permute-start.34 = (bf16[4,256,384]{2,1,0:T(8,128)(2,1)S(1)}, bf16[4,256,384]{2,1,0:T(8,128)(2,1)}, u32[]{:S(2)}, u32[]{:S(2)}) collective-permute-start(bf16[4,256,384]{2,1,0:T(8,128)(2,1)S(1)} %collective-permute-done.30.refs_2_), channel_id=1, source_target_pairs={{0,1},{1,0},{2,3},{3,2},{4,5},{5,4},{6,7},{7,6},{8,9},{9,8},{10,11... | collective-permute-start | bytes 2359304 | tf_op jit(solution)/shard_map/ppermute | solution.py:308
  152.2 27.5 %collective-permute-start.35 = (bf16[4,256,384]{2,1,0:T(8,128)(2,1)}, bf16[4,256,384]{2,1,0:T(8,128)(2,1)}, u32[]{:S(2)}, u32[]{:S(2)}) collective-permute-start(bf16[4,256,384]{2,1,0:T(8,128)(2,1)} %collective-permute-done.31.refs_3_), channel_id=1, source_target_pairs={{0,1},{1,0},{2,3},{3,2},{4,5},{5,4},{6,7},{7,6},{8,9},{9,8},{10,11... | collective-permute-start | bytes 2359304 | tf_op jit(solution)/shard_map/ppermute | solution.py:308
  152.3 27.5 %collective-permute-start.36 = (bf16[4,256,384]{2,1,0:T(8,128)(2,1)}, bf16[4,256,384]{2,1,0:T(8,128)(2,1)}, u32[]{:S(2)}, u32[]{:S(2)}) collective-permute-start(bf16[4,256,384]{2,1,0:T(8,128)(2,1)} %collective-permute-done.32.refs_4_), channel_id=1, source_target_pairs={{0,1},{1,0},{2,3},{3,2},{4,5},{5,4},{6,7},{7,6},{8,9},{9,8},{10,11... | collective-permute-start | bytes 2359304 | tf_op jit(solution)/shard_map/ppermute | solution.py:308
  156.4 14.8 %collective-permute-start.18 = (bf16[2,256,512]{2,1,0:T(8,128)(2,1)S(1)}, bf16[2,256,512]{2,1,0:T(8,128)(2,1)S(1)}, u32[]{:S(2)}, u32[]{:S(2)}) collective-permute-start(bf16[2,256,512]{2,1,0:T(8,128)(2,1)S(1)} %pad_maximum_fusion.4), channel_id=1, source_target_pairs={{0,2},{1,3},{2,4},{3,5},{4,6},{5,7},{6,0},{7,1},{8,10},{9,11},{10,... | collective-permute-start | bytes 1572872 | tf_op jit(solution)/shard_map/ppermute | solution.py:304
  (26 other events, 200.9 us)
